TPU v7x, 128 devices: a whole 4x4x4 slice. The times are simulated.
128 devices in a mesh: dp: 4 (over z), fsdp: 32 (over y, x, core).
Axes of the slice: x: 4, y: 4, z: 4, core: 2. Of those that a mesh axis runs over, the one named last changes fastest.
Arguments:
- layer_input: bfloat16 [32768, 768], P(('dp', 'fsdp')), may hold values from -6 to 6
- segments: int32 [128, 256], P(('dp', 'fsdp')), may hold values from 0 to 1, never falling along the last dimension, each value on 1 to 192 neighbouring positions
- norm_gain: bfloat16 [2, 2, 768], P(None, None, ('dp', 'fsdp')), may hold values from 0.25 to 1.75
- norm_bias: bfloat16 [2, 2, 768], P(None, None, ('dp', 'fsdp')), may hold values from -1.75 to 1.75
- query_weight: bfloat16 [2, 768, 768], P(None, ('dp', 'fsdp')), may hold values from -0.21875 to 0.21875
- query_bias: bfloat16 [2, 768], P(None, ('dp', 'fsdp')), may hold values from -1.75 to 1.75
- keyval_weight: bfloat16 [768, 128], P(('dp', 'fsdp')), may hold values from -0.21875 to 0.21875
- output_weight: bfloat16 [2, 768, 768], P(None, None, ('dp', 'fsdp')), may hold values from -1.25 to 1.25
- output_bias: bfloat16 [2, 768], P(None, ('dp', 'fsdp')), may hold values from -1.75 to 1.75
- upward_weight: bfloat16 [2, 768, 3072], P(None, None, ('dp', 'fsdp')), may hold values from -0.21875 to 0.21875
- upward_bias: bfloat16 [2, 3072], P(None, ('dp', 'fsdp')), may hold values from -1.75 to 1.75
- downward_weight: bfloat16 [2, 3072, 768], P(None, None, ('dp', 'fsdp')), may hold values from -0.109375 to 0.109375
- downward_bias: bfloat16 [2, 768], P(None, ('dp', 'fsdp')), may hold values from -1.75 to 1.75
- cotangent: bfloat16 [32768, 768], P(('dp', 'fsdp')), may hold values from -24 to 24
Outputs:
- block_output: bfloat16 [32768, 768], P(('dp', 'fsdp'))
- input_grad: bfloat16 [32768, 768], P(('dp', 'fsdp'))
- grad_norm_gain: float32 [2, 2, 768], P(None, None, ('dp', 'fsdp'))
- grad_norm_bias: float32 [2, 2, 768], P(None, None, ('dp', 'fsdp'))
- grad_query_weight: float32 [2, 768, 768], P(None, ('dp', 'fsdp'))
- grad_query_bias: float32 [2, 768], P(None, ('dp', 'fsdp'))
- grad_keyval_weight: float32 [768, 128], P(('dp', 'fsdp'))
- grad_output_weight: float32 [2, 768, 768], P(None, None, ('dp', 'fsdp'))
- grad_output_bias: float32 [2, 768], P(None, ('dp', 'fsdp'))
- grad_upward_weight: float32 [2, 768, 3072], P(None, None, ('dp', 'fsdp'))
- grad_upward_bias: float32 [2, 3072], P(None, ('dp', 'fsdp'))
- grad_downward_weight: float32 [2, 3072, 768], P(None, None, ('dp', 'fsdp'))
- grad_downward_bias: float32 [2, 768], P(None, ('dp', 'fsdp'))
Inputs may be any that keep to these rules, and one draw needn't show every extreme that they name: `segments`: within one device's row document numbers never fall; every number appears; each document holds 64 to 192 tokens.
All inputs are finite; a program needn't handle non-finite values.
Results may differ from a plain program's by a relative error of at most 0.014.
Values may be sent and summed in bfloat16 or wider, within the bound.
A program may use at most 192 MiB of HBM per device.

v0:
```python
import jax
import jax.numpy as jnp
from jax import lax
from jax.sharding import PartitionSpec as P

H = 12
HD = 64
D = 768


norm_epsilon = 1e-05
masked_score = -1e30
rotary_base = 10000.0
root_half = 0.7071067811865476
inverse_root_tau = 0.3989422804014327


def product(left, right):
    return jnp.dot(left, right, preferred_element_type=jnp.float32)


def product_tn(left, right):
    return lax.dot_general(
        left, right, (((0,), (0,)), ((), ())), preferred_element_type=jnp.float32
    )


def product_nt(left, right):
    return lax.dot_general(
        left, right, (((1,), (1,)), ((), ())), preferred_element_type=jnp.float32
    )


def column_sums(matrix):
    return jnp.sum(matrix.astype(jnp.float32), axis=0)


def doc_layout(doc_row):
    places = jnp.arange(doc_row.shape[0], dtype=jnp.int32)
    earlier = jnp.sum((doc_row[None, :] < doc_row[:, None]).astype(jnp.int32), axis=1)
    same_doc = doc_row[None, :] == doc_row[:, None]
    return (places - earlier, same_doc & (places[None, :] <= places[:, None]))


def rotary_tables(positions):
    half_width = HD // 8
    frequency = rotary_base ** (
        -(jnp.arange(half_width, dtype=jnp.float32) * 2.0) / (2 * half_width)
    )
    angles = positions.astype(jnp.float32)[:, None] * frequency[None, :]
    angles = jnp.concatenate([angles, angles], axis=1)
    return (jnp.cos(angles), jnp.sin(angles))


def rotate(values, cosine, sine):
    rot_width = cosine.shape[-1]
    half_width = rot_width // 2
    leading = values[..., :rot_width]
    turned = jnp.concatenate([-leading[..., half_width:], leading[..., :half_width]], axis=-1)
    return jnp.concatenate([leading * cosine + turned * sine, values[..., rot_width:]], axis=-1)


def rotate_back(gradient, cosine, sine):
    rot_width = cosine.shape[-1]
    half_width = rot_width // 2
    leading = gradient[..., :rot_width]
    with_sine = leading * sine
    turned = jnp.concatenate([with_sine[..., half_width:], -with_sine[..., :half_width]], axis=-1)
    return jnp.concatenate([leading * cosine + turned, gradient[..., rot_width:]], axis=-1)


def gelu_slope(hidden):
    return (
        0.5 * (1.0 + lax.erf(hidden * root_half))
        + hidden * jnp.exp(-0.5 * hidden * hidden) * inverse_root_tau
    )


def norm_parts(residual, gain_row, bias_row):
    centred = residual - jnp.mean(residual, axis=-1, keepdims=True)
    inverse = lax.rsqrt(jnp.mean(centred * centred, axis=-1, keepdims=True) + norm_epsilon)
    normed = centred * inverse
    return (normed * gain_row.astype(jnp.float32) + bias_row.astype(jnp.float32), normed, inverse)


def norm_back(gradient, normed, inverse, gain_row):
    scaled = gradient * gain_row.astype(jnp.float32)
    centred = (
        scaled
        - jnp.mean(scaled, axis=-1, keepdims=True)
        - normed * jnp.mean(scaled * normed, axis=-1, keepdims=True)
    )
    return (inverse * centred, jnp.sum(gradient * normed, axis=0), jnp.sum(gradient, axis=0))


def layer_front(residual, weights, cosine, sine):
    attn_in, normed_a, inverse_a = norm_parts(residual, weights[0][0], weights[1][0])
    mlp_in, normed_m, inverse_m = norm_parts(residual, weights[0][1], weights[1][1])
    attn_low = attn_in.astype(jnp.bfloat16)
    mlp_low = mlp_in.astype(jnp.bfloat16)
    queries = product(attn_low, weights[2]) + weights[3].astype(jnp.float32)
    queries = rotate(queries.reshape(-1, H, HD), cosine[:, None, :], sine[:, None, :]).astype(
        jnp.bfloat16
    )
    return (attn_low, mlp_low, queries, (normed_a, inverse_a, normed_m, inverse_m))


def make_shared(attn_low, keyval_w, cosine, sine):
    keyval = product(attn_low, keyval_w)
    return (
        rotate(keyval[:, :HD], cosine, sine).astype(jnp.bfloat16),
        keyval[:, HD:].astype(jnp.bfloat16),
    )


def score_block(queries, key_rows, allowed):
    raw_scores = jnp.einsum(
        "qhd,kd->hqk", queries, key_rows, preferred_element_type=jnp.float32
    ) * HD ** (-0.5)
    return jnp.where(allowed[None], raw_scores, masked_score)


def attend(queries, key_rows, value_rows, allowed):
    scores = score_block(queries, key_rows, allowed)
    top_score = jnp.max(scores, axis=-1, keepdims=True)
    exponent = jnp.exp(scores - top_score)
    total = jnp.sum(exponent, axis=-1, keepdims=True)
    prob_low = (exponent / total).astype(jnp.bfloat16)
    mixed = jnp.einsum("hqk,kd->qhd", prob_low, value_rows, preferred_element_type=jnp.float32)
    return (mixed.reshape(-1, D).astype(jnp.bfloat16), top_score + jnp.log(total))


def feed_forward(mlp_low, upward_w, upward_b, downward_w, downward_b):
    hidden = product(mlp_low, upward_w) + upward_b.astype(jnp.float32)
    activated = jax.nn.gelu(hidden, approximate=False).astype(jnp.bfloat16)
    return product(activated, downward_w) + downward_b.astype(jnp.float32)


def layer_forward(residual, weights, shared, cosine, sine, allowed):
    attn_low, mlp_low, queries, norm_stats = layer_front(residual, weights, cosine, sine)
    if shared is None:
        shared = make_shared(attn_low, weights[10], cosine, sine)
    mixed, log_total = attend(queries, shared[0], shared[1], allowed)
    attention = product(mixed, weights[4]) + weights[5].astype(jnp.float32)
    feed_out = feed_forward(mlp_low, weights[6], weights[7], weights[8], weights[9])
    return (residual + attention + feed_out, log_total, shared)


def layer_backward(residual, weights, shared, log_total, grad_out, cosine, sine, allowed):
    attn_low, mlp_low, queries, norm_stats = layer_front(residual, weights, cosine, sine)
    key_rows, value_rows = shared
    probs = jnp.exp(score_block(queries, key_rows, allowed) - log_total)
    prob_low = probs.astype(jnp.bfloat16)
    mixed = jnp.einsum("hqk,kd->qhd", prob_low, value_rows, preferred_element_type=jnp.float32)
    mixed = mixed.reshape(-1, D).astype(jnp.bfloat16)
    hidden = product(mlp_low, weights[6]) + weights[7].astype(jnp.float32)
    activated = jax.nn.gelu(hidden, approximate=False).astype(jnp.bfloat16)
    grad_low = grad_out.astype(jnp.bfloat16)
    grad_branch_bias = column_sums(grad_low)
    grad_mixed = product_nt(grad_low, weights[4]).astype(jnp.bfloat16).reshape(-1, H, HD)
    grad_probs = jnp.einsum(
        "qhd,kd->hqk", grad_mixed, value_rows, preferred_element_type=jnp.float32
    )
    grad_values = jnp.einsum(
        "hqk,qhd->kd", prob_low, grad_mixed, preferred_element_type=jnp.float32
    )
    grad_scores = probs * (grad_probs - jnp.sum(probs * grad_probs, axis=-1, keepdims=True))
    grad_scores = grad_scores.astype(jnp.bfloat16)
    scale = HD ** (-0.5)
    grad_queries = (
        jnp.einsum("hqk,kd->qhd", grad_scores, key_rows, preferred_element_type=jnp.float32) * scale
    )
    grad_keys = (
        jnp.einsum("hqk,qhd->kd", grad_scores, queries, preferred_element_type=jnp.float32) * scale
    )
    grad_queries = (
        rotate_back(grad_queries, cosine[:, None, :], sine[:, None, :])
        .reshape(-1, D)
        .astype(jnp.bfloat16)
    )
    grad_hidden = (product_nt(grad_low, weights[8]) * gelu_slope(hidden)).astype(jnp.bfloat16)
    grad_attn_in = product_nt(grad_queries, weights[2])
    grad_mlp_in = product_nt(grad_hidden, weights[6])
    matrices = (
        product_tn(attn_low, grad_queries),
        column_sums(grad_queries),
        product_tn(mixed, grad_low),
        grad_branch_bias,
        product_tn(mlp_low, grad_hidden),
        column_sums(grad_hidden),
        product_tn(activated, grad_low),
        grad_branch_bias,
    )
    return (grad_attn_in, grad_mlp_in, norm_stats, grad_keys, grad_values, matrices, attn_low)


def finish_norms(residual_grad, grad_attn_in, grad_mlp_in, norm_stats, norm_g):
    back_a, gain_a, bias_a = norm_back(grad_attn_in, norm_stats[0], norm_stats[1], norm_g[0])
    back_m, gain_m, bias_m = norm_back(grad_mlp_in, norm_stats[2], norm_stats[3], norm_g[1])
    return (
        residual_grad + back_a + back_m,
        jnp.stack([gain_a, gain_m]),
        jnp.stack([bias_a, bias_m]),
    )


def on_device(
    layer_input,
    segments,
    norm_gain,
    norm_bias,
    query_weight,
    query_bias,
    keyval_weight,
    output_weight,
    output_bias,
    upward_weight,
    upward_bias,
    downward_weight,
    downward_bias,
    cotangent,
):
    positions, allowed = doc_layout(segments[0])
    cosine, sine = rotary_tables(positions)
    producer_set = (
        lax.all_gather(norm_gain[0], ("dp", "fsdp"), axis=1, tiled=True),
        lax.all_gather(norm_bias[0], ("dp", "fsdp"), axis=1, tiled=True),
        lax.all_gather(query_weight[0], ("dp", "fsdp"), axis=0, tiled=True),
        lax.all_gather(query_bias[0], ("dp", "fsdp"), axis=0, tiled=True),
        lax.all_gather(output_weight[0], ("dp", "fsdp"), axis=1, tiled=True),
        lax.all_gather(output_bias[0], ("dp", "fsdp"), axis=0, tiled=True),
        lax.all_gather(upward_weight[0], ("dp", "fsdp"), axis=1, tiled=True),
        lax.all_gather(upward_bias[0], ("dp", "fsdp"), axis=0, tiled=True),
        lax.all_gather(downward_weight[0], ("dp", "fsdp"), axis=1, tiled=True),
        lax.all_gather(downward_bias[0], ("dp", "fsdp"), axis=0, tiled=True),
        lax.all_gather(keyval_weight, ("dp", "fsdp"), axis=0, tiled=True),
    )
    residual = layer_input.astype(jnp.float32)
    middle, log_first, shared = layer_forward(residual, producer_set, None, cosine, sine, allowed)
    reuser_set = (
        lax.all_gather(norm_gain[1], ("dp", "fsdp"), axis=1, tiled=True),
        lax.all_gather(norm_bias[1], ("dp", "fsdp"), axis=1, tiled=True),
        lax.all_gather(query_weight[1], ("dp", "fsdp"), axis=0, tiled=True),
        lax.all_gather(query_bias[1], ("dp", "fsdp"), axis=0, tiled=True),
        lax.all_gather(output_weight[1], ("dp", "fsdp"), axis=1, tiled=True),
        lax.all_gather(output_bias[1], ("dp", "fsdp"), axis=0, tiled=True),
        lax.all_gather(upward_weight[1], ("dp", "fsdp"), axis=1, tiled=True),
        lax.all_gather(upward_bias[1], ("dp", "fsdp"), axis=0, tiled=True),
        lax.all_gather(downward_weight[1], ("dp", "fsdp"), axis=1, tiled=True),
        lax.all_gather(downward_bias[1], ("dp", "fsdp"), axis=0, tiled=True),
    )
    last_resid, log_second, shared = layer_forward(
        middle, reuser_set, shared, cosine, sine, allowed
    )
    reuser_back = (
        lax.all_gather(norm_gain[1], ("dp", "fsdp"), axis=1, tiled=True),
        lax.all_gather(norm_bias[1], ("dp", "fsdp"), axis=1, tiled=True),
        lax.all_gather(query_weight[1], ("dp", "fsdp"), axis=0, tiled=True),
        lax.all_gather(query_bias[1], ("dp", "fsdp"), axis=0, tiled=True),
        lax.all_gather(output_weight[1], ("dp", "fsdp"), axis=1, tiled=True),
        lax.all_gather(output_bias[1], ("dp", "fsdp"), axis=0, tiled=True),
        lax.all_gather(upward_weight[1], ("dp", "fsdp"), axis=1, tiled=True),
        lax.all_gather(upward_bias[1], ("dp", "fsdp"), axis=0, tiled=True),
        lax.all_gather(downward_weight[1], ("dp", "fsdp"), axis=1, tiled=True),
        lax.all_gather(downward_bias[1], ("dp", "fsdp"), axis=0, tiled=True),
    )
    grad_out = cotangent.astype(jnp.float32)
    grad_attn_in, grad_mlp_in, norm_stats, keys_two, values_two, mats_two, unused = layer_backward(
        middle, reuser_back, shared, log_second, grad_out, cosine, sine, allowed
    )
    grad_middle, gains_two, biases_two = finish_norms(
        grad_out, grad_attn_in, grad_mlp_in, norm_stats, reuser_back[0]
    )
    sums_two = (
        lax.psum_scatter(gains_two, ("dp", "fsdp"), scatter_dimension=1, tiled=True),
        lax.psum_scatter(biases_two, ("dp", "fsdp"), scatter_dimension=1, tiled=True),
        lax.psum_scatter(mats_two[0], ("dp", "fsdp"), scatter_dimension=0, tiled=True),
        lax.psum_scatter(mats_two[1], ("dp", "fsdp"), scatter_dimension=0, tiled=True),
        lax.psum_scatter(mats_two[2], ("dp", "fsdp"), scatter_dimension=1, tiled=True),
        lax.psum_scatter(mats_two[3], ("dp", "fsdp"), scatter_dimension=0, tiled=True),
        lax.psum_scatter(mats_two[4], ("dp", "fsdp"), scatter_dimension=1, tiled=True),
        lax.psum_scatter(mats_two[5], ("dp", "fsdp"), scatter_dimension=0, tiled=True),
        lax.psum_scatter(mats_two[6], ("dp", "fsdp"), scatter_dimension=1, tiled=True),
        lax.psum_scatter(mats_two[7], ("dp", "fsdp"), scatter_dimension=0, tiled=True),
    )
    producer_back = (
        lax.all_gather(norm_gain[0], ("dp", "fsdp"), axis=1, tiled=True),
        lax.all_gather(norm_bias[0], ("dp", "fsdp"), axis=1, tiled=True),
        lax.all_gather(query_weight[0], ("dp", "fsdp"), axis=0, tiled=True),
        lax.all_gather(query_bias[0], ("dp", "fsdp"), axis=0, tiled=True),
        lax.all_gather(output_weight[0], ("dp", "fsdp"), axis=1, tiled=True),
        lax.all_gather(output_bias[0], ("dp", "fsdp"), axis=0, tiled=True),
        lax.all_gather(upward_weight[0], ("dp", "fsdp"), axis=1, tiled=True),
        lax.all_gather(upward_bias[0], ("dp", "fsdp"), axis=0, tiled=True),
        lax.all_gather(downward_weight[0], ("dp", "fsdp"), axis=1, tiled=True),
        lax.all_gather(downward_bias[0], ("dp", "fsdp"), axis=0, tiled=True),
        lax.all_gather(keyval_weight, ("dp", "fsdp"), axis=0, tiled=True),
    )
    grad_attn_in, grad_mlp_in, norm_stats, keys_one, values_one, mats_one, attn_low = (
        layer_backward(
            residual, producer_back, shared, log_first, grad_middle, cosine, sine, allowed
        )
    )
    grad_keys = rotate_back(keys_one + keys_two, cosine, sine)
    grad_shared = jnp.concatenate([grad_keys, values_one + values_two], axis=1).astype(jnp.bfloat16)
    grad_attn_in = grad_attn_in + product_nt(grad_shared, producer_back[10])
    grad_input, gains_one, biases_one = finish_norms(
        grad_middle, grad_attn_in, grad_mlp_in, norm_stats, producer_back[0]
    )
    sums_one = (
        lax.psum_scatter(gains_one, ("dp", "fsdp"), scatter_dimension=1, tiled=True),
        lax.psum_scatter(biases_one, ("dp", "fsdp"), scatter_dimension=1, tiled=True),
        lax.psum_scatter(mats_one[0], ("dp", "fsdp"), scatter_dimension=0, tiled=True),
        lax.psum_scatter(mats_one[1], ("dp", "fsdp"), scatter_dimension=0, tiled=True),
        lax.psum_scatter(mats_one[2], ("dp", "fsdp"), scatter_dimension=1, tiled=True),
        lax.psum_scatter(mats_one[3], ("dp", "fsdp"), scatter_dimension=0, tiled=True),
        lax.psum_scatter(mats_one[4], ("dp", "fsdp"), scatter_dimension=1, tiled=True),
        lax.psum_scatter(mats_one[5], ("dp", "fsdp"), scatter_dimension=0, tiled=True),
        lax.psum_scatter(mats_one[6], ("dp", "fsdp"), scatter_dimension=1, tiled=True),
        lax.psum_scatter(mats_one[7], ("dp", "fsdp"), scatter_dimension=0, tiled=True),
        lax.psum_scatter(
            product_tn(attn_low, grad_shared), ("dp", "fsdp"), scatter_dimension=0, tiled=True
        ),
    )
    block_output = last_resid.astype(jnp.bfloat16)
    input_grad = grad_input.astype(jnp.bfloat16)
    return (
        block_output,
        input_grad,
        jnp.stack([sums_one[0], sums_two[0]]),
        jnp.stack([sums_one[1], sums_two[1]]),
        jnp.stack([sums_one[2], sums_two[2]]),
        jnp.stack([sums_one[3], sums_two[3]]),
        sums_one[10],
        jnp.stack([sums_one[4], sums_two[4]]),
        jnp.stack([sums_one[5], sums_two[5]]),
        jnp.stack([sums_one[6], sums_two[6]]),
        jnp.stack([sums_one[7], sums_two[7]]),
        jnp.stack([sums_one[8], sums_two[8]]),
        jnp.stack([sums_one[9], sums_two[9]]),
    )


def solution(mesh):
    in_specs = (
        P(("dp", "fsdp"), None),
        P(("dp", "fsdp"), None),
        P(None, None, ("dp", "fsdp")),
        P(None, None, ("dp", "fsdp")),
        P(None, ("dp", "fsdp"), None),
        P(None, ("dp", "fsdp")),
        P(("dp", "fsdp"), None),
        P(None, None, ("dp", "fsdp")),
        P(None, ("dp", "fsdp")),
        P(None, None, ("dp", "fsdp")),
        P(None, ("dp", "fsdp")),
        P(None, None, ("dp", "fsdp")),
        P(None, ("dp", "fsdp")),
        P(("dp", "fsdp"), None),
    )
    out_specs = (
        P(("dp", "fsdp"), None),
        P(("dp", "fsdp"), None),
        P(None, None, ("dp", "fsdp")),
        P(None, None, ("dp", "fsdp")),
        P(None, ("dp", "fsdp"), None),
        P(None, ("dp", "fsdp")),
        P(("dp", "fsdp"), None),
        P(None, None, ("dp", "fsdp")),
        P(None, ("dp", "fsdp")),
        P(None, None, ("dp", "fsdp")),
        P(None, ("dp", "fsdp")),
        P(None, None, ("dp", "fsdp")),
        P(None, ("dp", "fsdp")),
    )
    return jax.shard_map(
        on_device, mesh=mesh, in_specs=in_specs, out_specs=out_specs, check_vma=False
    )
```

profile of v0, /device:TPU:1, one launch (start us, length us, event | category | flops | bytes accessed | tf_op | source)
XLA Modules:
  0.0 1854.0 jit_solution(4720758188522826916)
XLA Ops:
  20.2 38.8 %all-gather.11 = bf16[1,2,768]{1,0,2:T(2,128)(2,1)S(1)} all-gather(bf16[1,2,6]{1,0,2:T(2,128)(2,1)S(1)} %copy.145), channel_id=13, replica_groups=mesh['dp'=4,'fsdp'=32] {'dp','fsdp'}, dimensions={2}, use_global_device_ids=true | all-gather | bytes 3096 | tf_op jit(solution)/shard_map/all_gather | solution.py:242
  65.0 33.3 %all-gather.10 = bf16[1,2,768]{1,0,2:T(2,128)(2,1)S(1)} all-gather(bf16[1,2,6]{1,0,2:T(2,128)(2,1)S(1)} %copy.144), channel_id=12, replica_groups=mesh['dp'=4,'fsdp'=32] {'dp','fsdp'}, dimensions={2}, use_global_device_ids=true | all-gather | bytes 3096 | tf_op jit(solution)/shard_map/all_gather | solution.py:241
  98.5 33.3 %all-gather.1 = bf16[1,2,768]{1,0,2:T(2,128)(2,1)S(1)} all-gather(bf16[1,2,6]{1,0,2:T(2,128)(2,1)S(1)} %copy.143), channel_id=3, replica_groups=mesh['dp'=4,'fsdp'=32] {'dp','fsdp'}, dimensions={2}, use_global_device_ids=true | all-gather | bytes 3096 | tf_op jit(solution)/shard_map/all_gather | solution.py:227
  136.6 33.5 %all-gather = bf16[1,2,768]{1,0,2:T(2,128)(2,1)S(1)} all-gather(bf16[1,2,6]{1,0,2:T(2,128)(2,1)S(1)} %copy.142), channel_id=2, replica_groups=mesh['dp'=4,'fsdp'=32] {'dp','fsdp'}, dimensions={2}, use_global_device_ids=true | all-gather | bytes 3096 | tf_op jit(solution)/shard_map/all_gather | solution.py:226
  175.3 33.4 %all-gather.20 = bf16[128,6,128]{2,1,0:T(8,128)(2,1)S(1)} all-gather(bf16[1,6,128]{2,1,0:T(8,128)(2,1)S(1)} %bitcast.274), channel_id=1, replica_groups=mesh['dp'=4,'fsdp'=32] {'dp','fsdp'}, dimensions={0}, use_global_device_ids=true | all-gather | bytes 198144 | tf_op jit(solution)/shard_map/all_gather | solution.py:236
  216.5 65.5 %all-reduce.32 = (bf16[3072]{0:T(1024)(128)(2,1)S(1)}, bf16[3072]{0:T(1024)(128)(2,1)S(1)}, bf16[768]{0:T(1024)(128)(2,1)S(1)}, bf16[768]{0:T(1024)(128)(2,1)S(1...) all-reduce(bf16[3072]{0:T(1024)(128)(2,1)S(1)} %dynamic-update-slic, ...), channel_id=19, replica_groups=mesh['dp'=4,'fsdp'=32] {'dp','fsdp'}, use_global_device_ids=true, to_apply=%add.6 | all-reduce | flops 10752 | bytes 43008
  306.2 19.8 %copy.102 = bf16[1,3072,768]{2,1,0:T(8,128)(2,1)} copy(bf16[1,3072,768]{1,0,2:T(2,128)(2,1)} %all-gather.36.cloned.1.call-done) | data formatting | bytes 9437184 | tf_op jit(solution)/shard_map/all_gather | solution.py:234
  326.0 26.7 %all-gather.34.cloned.1.call-done = bf16[1,768,3072]{1,2,0:T(8,128)(2,1)} async-done(((bf16[1,768,24]{1,2,0:T(8,128)(2,1)}), bf16[1,768,3072]{1,2,0:T(8,128)(2,1)}) %all-gather.34.cloned.1.call-update) | async-done | bytes 4718608 | tf_op jit(solution)/shard_map/all_gather | solution.py:232
  352.7 11.1 fusion.42
  366.2 52.2 %all-gather.38.cloned.1.call-done = bf16[1,768,768]{2,0,1:T(2,128)(2,1)} async-done(((bf16[1,6,768]{2,0,1:T(2,128)(2,1)}), bf16[1,768,768]{2,0,1:T(2,128)(2,1)}) %all-gather.38.cloned.1.call-update) | async-done | bytes 1179664 | tf_op jit(solution)/shard_map/all_gather | solution.py:243
  428.5 61.7 %all-gather.44.cloned.1.call-done = bf16[1,3072,768]{1,0,2:T(2,128)(2,1)} async-done(((bf16[1,3072,6]{1,0,2:T(2,128)(2,1)}), bf16[1,3072,768]{1,0,2:T(2,128)(2,1)}) %all-gather.44.cloned.1.call-update) | async-done | bytes 4718608 | tf_op jit(solution)/shard_map/all_gather | solution.py:249
  490.2 19.7 %copy.108 = bf16[1,3072,768]{2,1,0:T(8,128)(2,1)} copy(bf16[1,3072,768]{1,0,2:T(2,128)(2,1)} %all-gather.44.cloned.1.call-done) | data formatting | bytes 9437184 | tf_op jit(solution)/shard_map/all_gather | solution.py:249
  511.5 46.9 %all-gather.42.cloned.1.call-done = bf16[1,768,3072]{1,2,0:T(8,128)(2,1)} async-done(((bf16[1,768,24]{1,2,0:T(8,128)(2,1)}), bf16[1,768,3072]{1,2,0:T(8,128)(2,1)}) %all-gather.42.cloned.1.call-update) | async-done | bytes 4718608 | tf_op jit(solution)/shard_map/all_gather | solution.py:247
  558.5 11.0 fusion.45
  636.4 414.8 %fusion.180 = (f32[8,768]{1,0:T(8,128)}, f32[8,768]{1,0:T(8,128)}, f32[768,8]{0,1:T(8,128)}, f32[768,8]{0,1:T(8,128)}, f32[3072,8]{0,1:T(8,128)}, /*index=5*/f32[3072,8]{0,1:T(8,128)}) fusion(f32[768,768]{1,0:T(8,128)} %fusion.157, f32[768,768]{1,0:T(8,128)} %fusion.195, f32[768,768]{0,1:T(8,128)} %fusion.197, f32[768,768]{0,1:T(8,128)} %fusion.196, ...), kind=kCustom, calls=%all-reduce-scatter.6 | all-reduce-scatter fusion | flops 9437185 | bytes 28606464
  1083.8 8.4 collective-permute-start.54
  1282.1 64.3 %all-reduce.31 = (f32[2,768]{1,0:T(2,128)S(1)}, f32[2,768]{1,0:T(2,128)S(1)}, f32[2,768]{1,0:T(2,128)S(1)}, f32[2,768]{1,0:T(2,128)S(1)}, f32[768]{0:T(1024)S(1)...) all-reduce(f32[2,768]{1,0:T(2,128)S(1)} %get-tuple-element.195, ...), channel_id=23, replica_groups=mesh['dp'=4,'fsdp'=32] {'dp','fsdp'}, use_global_device_ids=true, to_apply=%region_24.25.clone | all-reduce | flops 15360 | bytes 122880
  1557.1 27.2 %concatenate.69 = f32[262,768]{1,0:T(8,128)S(1)} concatenate(f32[6,768]{1,0:T(8,128)} %copy-done.169, f32[8,768]{1,0:T(8,128)} %copy-done.170, f32[8,768]{1,0:T(8,128)} %copy-done.171, f32[8,768]{1,0:T(8,128)} %copy-done.172, f32[8,768]{1,0:T(8,128)} %collective-permute-done.59, f32[8,768]{1,0:T(8,128)} %collective-permute-done.58, f32[8,768]{1,0:T(8,128)} %collective-permute-done.57, ...), dimensions={0} | concatenate | bytes 1609728
  1584.4 27.2 %concatenate.68 = f32[262,768]{1,0:T(8,128)S(1)} concatenate(f32[6,768]{1,0:T(8,128)} %copy-done.168, f32[8,768]{1,0:T(8,128)} %copy-done.191, f32[8,768]{1,0:T(8,128)} %copy-done.192, f32[8,768]{1,0:T(8,128)} %copy-done.193, f32[8,768]{1,0:T(8,128)} %copy-done.194, f32[8,768]{1,0:T(8,128)} %copy-done.195, f32[8,768]{1,0:T(8,128)} %copy-done.196, f32[8,768]{1,0:T(8,128)} %copy-done.197, ...), dimensions={0} | concatenate | bytes 1609728
  1629.0 8.3 collective-permute-start.149
  1655.5 25.7 %concatenate.71 = f32[768,262]{0,1:T(8,128)S(1)} concatenate(f32[768,6]{0,1:T(8,128)S(1)} %copy-done.167, f32[768,8]{0,1:T(8,128)S(1)} %copy-done.205, f32[768,8]{0,1:T(8,128)} %copy-done.207, f32[768,8]{0,1:T(8,128)} %copy-done.209, f32[768,8]{0,1:T(8,128)} %copy-done.211, f32[768,8]{0,1:T(8,128)} %copy-done.213, f32[768,8]{0,1:T(8,128)} %copy-done.215, f32[768,8]{0,1:T(8,128)} %copy-done.220, ...), dimensions={1} | concatenate | bytes 1609728
  1681.3 26.5 %concatenate.70 = f32[768,262]{0,1:T(8,128)S(1)} concatenate(f32[768,6]{0,1:T(8,128)S(1)} %copy-done.165, f32[768,8]{0,1:T(8,128)} %collective-permute-done.94, f32[768,8]{0,1:T(8,128)} %collective-permute-done.93, f32[768,8]{0,1:T(8,128)} %collective-permute-done.92, f32[768,8]{0,1:T(8,128)} %collective-permute-done.91, f32[768,8]{0,1:T(8,128)} %collective-permute-done.90, ...), dimensions={1} | concatenate | bytes 1609728
  1753.7 32.4 %concatenate.73 = f32[3072,262]{0,1:T(8,128)S(1)} concatenate(f32[3072,6]{0,1:T(8,128)} %copy-done.86, f32[3072,8]{0,1:T(8,128)S(1)} %collective-permute-done.190, f32[3072,8]{0,1:T(8,128)} %copy-done.85, f32[3072,8]{0,1:T(8,128)} %copy-done.87, f32[3072,8]{0,1:T(8,128)} %copy-done.88, f32[3072,8]{0,1:T(8,128)} %copy-done.89, f32[3072,8]{0,1:T(8,128)} %copy-done.90, ...), dimensions={1} | concatenate | bytes 6438912
  1786.1 55.0 %concatenate.72 = f32[3072,262]{0,1:T(8,128)} concatenate(f32[3072,6]{0,1:T(8,128)S(1)} %collective-permute-done.159, f32[3072,8]{0,1:T(8,128)} %copy-done.114, f32[3072,8]{0,1:T(8,128)} %copy-done.115, f32[3072,8]{0,1:T(8,128)} %copy-done.116, f32[3072,8]{0,1:T(8,128)} %copy-done.117, f32[3072,8]{0,1:T(8,128)} %copy-done.118, f32[3072,8]{0,1:T(8,128)} %copy-done.119, ...), dimensions={1} | concatenate | bytes 6438912
  (1141 shorter events, 657.1 us)
Async XLA Ops:
  7.2 276.2 %all-gather.30.cloned.1.call-start = ((), (), s32[]{:S(2)}) async-start(), calls=%async_computation.4 | async-start | bytes 2377728 | tf_op jit(solution)/shard_map/all_gather | solution.py:228
  8.7 280.0 %all-gather.40.cloned.1.call-start = ((), (), s32[]{:S(2)}) async-start(), calls=%async_computation.9 | async-start | bytes 2377728 | tf_op jit(solution)/shard_map/all_gather | solution.py:245
  10.2 285.4 %all-gather.32.cloned.1.call-start = ((), (), s32[]{:S(2)}) async-start(), calls=%async_computation.5 | async-start | bytes 2377728 | tf_op jit(solution)/shard_map/all_gather | solution.py:230
  11.0 295.2 %all-gather.36.cloned.1.call-start = ((), (), s32[]{:S(2)}) async-start(), calls=%async_computation.7 | async-start | bytes 9510912 | tf_op jit(solution)/shard_map/all_gather | solution.py:234
  12.8 339.9 %all-gather.34.cloned.1.call-start = ((), (), s32[]{:S(2)}) async-start(), calls=%async_computation.6 | async-start | bytes 4755456 | tf_op jit(solution)/shard_map/all_gather | solution.py:232
  14.3 404.1 %all-gather.38.cloned.1.call-start = ((), (), s32[]{:S(2)}) async-start(), calls=%async_computation.8 | async-start | bytes 2377728 | tf_op jit(solution)/shard_map/all_gather | solution.py:243
  14.9 475.4 %all-gather.44.cloned.1.call-start = ((), (), s32[]{:S(2)}) async-start(), calls=%async_computation.11 | async-start | bytes 9510912 | tf_op jit(solution)/shard_map/all_gather | solution.py:249
  15.6 542.8 %all-gather.42.cloned.1.call-start = ((), (), s32[]{:S(2)}) async-start(), calls=%async_computation.10 | async-start | bytes 4755456 | tf_op jit(solution)/shard_map/all_gather | solution.py:247
  16.4 1826.6 %all-reduce.36.cloned.1.call-start = ((), (), s32[]{:S(2)}) async-start(), calls=%async_computation.12 | async-start | bytes 786432
  593.2 1251.1 %reduce-scatter.21.cloned.1.call-start = ((), (), s32[]{:S(2)}) async-start(), calls=%async_computation.3 | async-start | bytes 9510912 | tf_op jit(solution)/shard_map/reduce_scatter | solution.py:281
  600.1 1244.1 %reduce-scatter.19.cloned.1.call-start = ((), (), s32[]{:S(2)}) async-start(), calls=%async_computation.2 | async-start | bytes 9510912 | tf_op jit(solution)/shard_map/reduce_scatter | solution.py:317
  1268.0 78.4 %collective-permute-start.110 = (f32[768,8]{0,1:T(8,128)S(1)}, f32[768,8]{0,1:T(8,128)S(1)}, u32[]{:S(2)}, u32[]{:S(2)}) collective-permute-start(f32[768,8]{0,1:T(8,128)S(1)} %copy-done.73), channel_id=1, source_target_pairs={{0,15},{1,16},{2,17},{3,18},{4,19},{5,20},{6,21},{7,22},{8,23},{9,... | collective-permute-start | bytes 73736
  1270.4 78.2 %collective-permute-start.109 = (f32[768,8]{0,1:T(8,128)S(1)}, f32[768,8]{0,1:T(8,128)S(1)}, u32[]{:S(2)}, u32[]{:S(2)}) collective-permute-start(f32[768,8]{0,1:T(8,128)S(1)} %copy-done.73), channel_id=1, source_target_pairs={{0,14},{1,15},{2,16},{3,17},{4,18},{5,19},{6,20},{7,21},{8,22},{9,... | collective-permute-start | bytes 73736
  1272.2 80.9 %collective-permute-start.108 = (f32[768,8]{0,1:T(8,128)S(1)}, f32[768,8]{0,1:T(8,128)S(1)}, u32[]{:S(2)}, u32[]{:S(2)}) collective-permute-start(f32[768,8]{0,1:T(8,128)S(1)} %copy-done.73), channel_id=1, source_target_pairs={{0,13},{1,14},{2,15},{3,16},{4,17},{5,18},{6,19},{7,20},{8,21},{9,... | collective-permute-start | bytes 73736
  1275.4 80.0 %collective-permute-start.107 = (f32[768,8]{0,1:T(8,128)S(1)}, f32[768,8]{0,1:T(8,128)S(1)}, u32[]{:S(2)}, u32[]{:S(2)}) collective-permute-start(f32[768,8]{0,1:T(8,128)S(1)} %copy-done.73), channel_id=1, source_target_pairs={{0,12},{1,13},{2,14},{3,15},{4,16},{5,17},{6,18},{7,19},{8,20},{9,... | collective-permute-start | bytes 73736
  1277.8 80.3 %collective-permute-start.106 = (f32[768,8]{0,1:T(8,128)S(1)}, f32[768,8]{0,1:T(8,128)S(1)}, u32[]{:S(2)}, u32[]{:S(2)}) collective-permute-start(f32[768,8]{0,1:T(8,128)S(1)} %copy-done.73), channel_id=1, source_target_pairs={{0,11},{1,12},{2,13},{3,14},{4,15},{5,16},{6,17},{7,18},{8,19},{9,... | collective-permute-start | bytes 73736
  1542.5 69.1 %collective-permute-start.163 = (f32[3072,8]{0,1:T(8,128)S(1)}, f32[3072,8]{0,1:T(8,128)S(1)}, u32[]{:S(2)}, u32[]{:S(2)}) collective-permute-start(f32[3072,8]{0,1:T(8,128)S(1)} %copy-done.44), channel_id=1, source_target_pairs={{0,4},{1,5},{2,6},{3,7},{4,8},{5,9},{6,10},{7,11},{8,12},{9,13},{1... | collective-permute-start | bytes 294920
  1546.1 68.3 %collective-permute-start.162 = (f32[3072,8]{0,1:T(8,128)S(1)}, f32[3072,8]{0,1:T(8,128)S(1)}, u32[]{:S(2)}, u32[]{:S(2)}) collective-permute-start(f32[3072,8]{0,1:T(8,128)S(1)} %copy-done.44), channel_id=1, source_target_pairs={{0,3},{1,4},{2,5},{3,6},{4,7},{5,8},{6,9},{7,10},{8,11},{9,12},{10... | collective-permute-start | bytes 294920
  1549.2 68.6 %collective-permute-start.161 = (f32[3072,8]{0,1:T(8,128)S(1)}, f32[3072,8]{0,1:T(8,128)}, u32[]{:S(2)}, u32[]{:S(2)}) collective-permute-start(f32[3072,8]{0,1:T(8,128)S(1)} %copy-done.44), channel_id=1, source_target_pairs={{0,2},{1,3},{2,4},{3,5},{4,6},{5,7},{6,8},{7,9},{8,10},{9,11},{10,... | collective-permute-start | bytes 294920
  1552.6 66.5 %collective-permute-start.160 = (f32[3072,8]{0,1:T(8,128)S(1)}, f32[3072,8]{0,1:T(8,128)}, u32[]{:S(2)}, u32[]{:S(2)}) collective-permute-start(f32[3072,8]{0,1:T(8,128)S(1)} %copy-done.44), channel_id=1, source_target_pairs={{0,1},{1,2},{2,3},{3,4},{4,5},{5,6},{6,7},{7,8},{8,9},{9,10},{10,1... | collective-permute-start | bytes 294920
  1555.1 66.8 %collective-permute-start.158 = (f32[3072,8]{0,1:T(8,128)}, f32[3072,8]{0,1:T(8,128)S(1)}, u32[]{:S(2)}, u32[]{:S(2)}) collective-permute-start(f32[3072,8]{0,1:T(8,128)} %get-tuple-element.125), channel_id=1, source_target_pairs={{0,31},{1,32},{2,33},{3,34},{4,35},{5,36},{6,37},{7,38},{8,39},{9,... | collective-permute-start | bytes 294920
  1638.7 69.1 %collective-permute-start.147 = (f32[3072,8]{0,1:T(8,128)}, f32[3072,8]{0,1:T(8,128)S(1)}, u32[]{:S(2)}, u32[]{:S(2)}) collective-permute-start(f32[3072,8]{0,1:T(8,128)} %get-tuple-element.125), channel_id=1, source_target_pairs={{0,20},{1,21},{2,22},{3,23},{4,24},{5,25},{6,26},{7,27},{8,28},{9,... | collective-permute-start | bytes 294920
  1640.0 69.1 %collective-permute-start.146 = (f32[3072,8]{0,1:T(8,128)}, f32[3072,8]{0,1:T(8,128)}, u32[]{:S(2)}, u32[]{:S(2)}) collective-permute-start(f32[3072,8]{0,1:T(8,128)} %get-tuple-element.125), channel_id=1, source_target_pairs={{0,19},{1,20},{2,21},{3,22},{4,23},{5,24},{6,25},{7,26},{8,27},{9,... | collective-permute-start | bytes 294920
  1649.1 66.5 %collective-permute-start.144 = (f32[3072,8]{0,1:T(8,128)}, f32[3072,8]{0,1:T(8,128)}, u32[]{:S(2)}, u32[]{:S(2)}) collective-permute-start(f32[3072,8]{0,1:T(8,128)} %get-tuple-element.125), channel_id=1, source_target_pairs={{0,17},{1,18},{2,19},{3,20},{4,21},{5,22},{6,23},{7,24},{8,25},{9,... | collective-permute-start | bytes 294920
  (450 other events, 21098.5 us)
Sparse Core Ops, SparseCore 0:
  11.6 68.9 all-gather.29
  84.1 62.6 all-gather.39
  149.8 62.6 all-gather.31
  216.0 68.2 all-gather.35
  287.8 64.8 all-gather.33
  355.5 62.7 all-gather.37
  422.0 68.2 all-gather.43
  493.8 64.5 all-gather.41
  593.3 141.4 all-reduce.35
  739.6 221.7 reduce-scatter.20
  966.4 215.0 reduce-scatter.18
where the time goes:
time: 1880 us; the launch traced here: 1850 us
  blocking collectives  717 us (38%)
  starting transfers between devices  497 us (26%)
  local copies, waits for them, and re-layouts  285 us (15%)
  waiting for transfers between devices  195 us (10%)
  matrix products  100 us (5%)
  other arithmetic  39.8 us (2%)
  between operations  20.5 us (1%)
    unnamed x3, blocking collectives  545 us
    unnamed x193, starting transfers between devices  496 us
    unnamed x584, local copies, waits for them, and re-layouts  219 us
    all_gather x1, waiting for transfers between devices, on_device(): lax.all_gather(downward_weight[1], ('dp', 'fsdp'), axis=1, tiled=True)  61.7 us
    all_gather x1, waiting for transfers between devices, on_device(): lax.all_gather(query_weight[1], ('dp', 'fsdp'), axis=0, tiled=True)  52.2 us
    all_gather x1, waiting for transfers between devices, on_device(): lax.all_gather(upward_weight[1], ('dp', 'fsdp'), axis=1, tiled=True)  46.9 us
    all_gather x1, blocking collectives, on_device(): lax.all_gather(norm_bias[1], ('dp', 'fsdp'), axis=1, tiled=True)  38.8 us
  transfers between devices with their start and end apart: 203, of which 6 were waited for; matrix products, arithmetic and copies ran while one was open for 43% of the time, Pallas kernels for 0%

commit v1 on v0

v1 whole, which is shorter than its diff:
```python
import functools

import jax
import jax.numpy as jnp
import numpy as np
from jax import lax
from jax.experimental import pallas as pl
from jax.experimental.pallas import tpu as pltpu
from jax.sharding import PartitionSpec as P

MESH = pl.DeviceIdType.MESH
F32 = jnp.float32
BF16 = jnp.bfloat16

H = 12
HD = 64
D = 768
FF = 3072
TOK = 256
HALF = 384
ROWS = 512
KV0, VEC0, Q0, O0, D0, U0 = 0, 16, 32, 80, 128, 320
CHUNK = 64

norm_epsilon = 1e-05
masked_score = -1e30
rotary_base = 10000.0
root_half = 0.7071067811865476
inverse_root_tau = 0.3989422804014327
scale = HD**-0.5


def place_constants():
    qod = np.zeros((288, 512), np.float32)
    kv = np.zeros((48, 512), np.float32)
    for s in range(8):
        for i in range(6):
            r = s * 6 + i
            qod[r, s * CHUNK + 22 + i] = 1
            qod[48 + r, s * CHUNK + 28 + i] = 1
            for g in range(4):
                qod[96 + 48 * g + r, s * CHUNK + 34 + 4 * i + g] = 1
            kv[r, s * CHUNK + 16 + i] = 1
    up = np.zeros((192, 192), np.float32)
    for h in range(2):
        for x in range(4):
            for j in range(24):
                up[h * 96 + x * 24 + j, x * 48 + h * 24 + j] = 1
    perm = np.zeros((768, 768), np.float32)
    for chip in range(16):
        for c in range(2):
            for j in range(24):
                perm[chip * 48 + c * 24 + j, c * 384 + chip * 24 + j] = 1
    spread48 = np.zeros((128, 768), np.float32)
    spread48[np.arange(768) % 48, np.arange(768)] = 1
    spread96 = np.zeros((128, 1536), np.float32)
    spread96[np.arange(1536) % 96, np.arange(1536)] = 1
    return qod, kv, up, perm, spread48, spread96, qod.T, kv.T, up.T


CONSTS = place_constants()


def nn(a, b):
    return jnp.dot(a, b, preferred_element_type=F32)


def nt(a, b):
    return lax.dot_general(a, b, (((1,), (1,)), ((), ())), preferred_element_type=F32)


def tn(a, b):
    return lax.dot_general(a, b, (((0,), (0,)), ((), ())), preferred_element_type=F32)


def ranges(lengths):
    at, out = 0, []
    for n in lengths:
        out.append((at, n))
        at += n
    return out


class Place:
    def __init__(self):
        self.z = lax.axis_index("dp")
        f = lax.axis_index("fsdp")
        self.y = f // 8
        self.x = (f // 2) % 4
        self.c = f % 2

    def dev(self, dz=0, dy=0, dx=0, dc=0):
        z = (self.z + dz) % 4
        y = (self.y + dy) % 4
        x = (self.x + dx) % 4
        c = (self.c + dc) % 2
        return (z, y * 8 + x * 2 + c)

    def along(self, axis, d):
        return self.dev(**{"d" + axis: d})

    def pos(self, axis):
        return getattr(self, axis)


class Ring:
    def __init__(self, me, axis, view, sems, many):
        self.me, self.axis, self.view, self.sems, self.many = me, axis, view, sems, many
        self.p = me.pos(axis)

    def _copy(self, to, src, dst, sem):
        return pltpu.make_async_remote_copy(
            src_ref=src,
            dst_ref=dst,
            send_sem=self.sems.at[0],
            recv_sem=self.sems.at[sem],
            device_id=self.me.along(self.axis, to),
            device_id_type=MESH,
        )

    def _await(self, ref, sem):
        pltpu.make_async_copy(ref, ref, self.sems.at[sem]).wait()

    def sent(self):
        self._await(self.many(3), 0)


class Gather(Ring):
    def _pass(self, to, k, h, sem):
        block = self.view(k % 4, h)
        self._copy(to, block, block, sem).start()

    def start(self):
        p = self.p
        self._pass(1, p, 0, 1)
        self._pass(-1, p, 1, 2)
        self._pass(1, p, 1, 3)
        self._pass(-1, p, 0, 3)

    def forward(self):
        p = self.p
        self._await(self.view((p + 3) % 4, 0), 1)
        self._pass(1, p + 3, 0, 4)
        self._await(self.view((p + 1) % 4, 1), 2)
        self._pass(-1, p + 1, 1, 4)

    def near(self):
        self._await(self.many(1), 3)

    def far(self):
        self._await(self.many(1), 4)

    def finish(self):
        self.near()
        self.far()
        self.sent()


class Scatter(Ring):
    def __init__(self, me, axis, view, sems, many, buf, leads, rows):
        super().__init__(me, axis, view, sems, many)
        self.buf, self.leads, self.rows = buf, leads, rows

    def _slot(self, j, h):
        ref = self.buf.at[j]
        n = self.rows[h]
        if n != ref.shape[-2]:
            ref = ref.at[tuple(slice(None) for _ in self.leads) + (pl.ds(0, n),)]
        return ref

    def _pass(self, to, k, h, slot, sem):
        self._copy(to, self.view(k % 4, h), self._slot(slot, h), sem).start()

    def _add(self, k, h, slots):
        target = self.view(k, h)
        srcs = [self._slot(s, h) for s in slots]

        def one(idx):
            total = target[idx].astype(F32)
            for s in srcs:
                total = total + s[idx].astype(F32)
            target[idx] = total.astype(BF16)

        if not self.leads:
            one((slice(None), slice(None)))
        else:

            @pl.loop(0, self.leads[0])
            def _(i):
                one((i,))

    def start_far(self):
        p = self.p
        self._pass(1, p + 2, 0, 0, 1)
        self._pass(-1, p + 2, 1, 1, 2)

    def start_near(self):
        p = self.p
        self._pass(1, p + 1, 1, 3, 3)
        self._pass(-1, p + 3, 0, 4, 3)

    def start(self):
        self.start_far()
        self.start_near()

    def forward(self):
        p = self.p
        self._await(self._slot(0, 0), 1)
        self._add((p + 1) % 4, 0, [0])
        self._pass(1, p + 1, 0, 2, 3)
        self._await(self._slot(1, 1), 2)
        self._add((p + 3) % 4, 1, [1])
        self._pass(-1, p + 3, 1, 5, 3)

    def finish(self):
        self._await(self.many(2), 3)
        self._add(self.p, 0, [2, 4])
        self._add(self.p, 1, [3, 5])
        self.sent()


def kernel(
    xin, seg, cot, w_gain, w_nbias, w_q, w_qb, w_kv, w_o, w_ob, w_up, w_ub, w_down, w_db, h_qod, h_kv, h_up, h_perm, h_s48, h_s96, h_qodT, h_kvT, h_upT,
    out_y, out_gx, out_v, out_u,
    W, chunk, rawu, got, gotu, vecs, ubv,
    X2, gl, seg2, cosT, sinT, mbias, n_, r_, h1, attn, mlp, kvT, k_, v_, qT, p_, mixT, mixed, act, slope,
    acc, glT, attnT, gm, gmT, dk, dv, gs, vg, ubg, g_, xs, xr,
    bA2, bB2, bO2, bU2, bV2, bD1, bD2, bA3, bB3, bO3, bU3, bV3, bD3, rgot, rgotu,
    c_qod, c_kv, c_up, c_perm, c_s48, c_s96, c_qodT, c_kvT, c_upT,
    const_sem, pair_send, pair_recv, line_sem, ag_sem, rs_sem,
):
    me = Place()
    z, y, x, c = me.z, me.y, me.x, me.c
    s_me = x * 2 + c

    consts = [(h_perm, c_perm), (h_qod, c_qod), (h_kv, c_kv), (h_up, c_up), (h_s48, c_s48), (h_s96, c_s96),
              (h_qodT, c_qodT), (h_kvT, c_kvT), (h_upT, c_upT)]
    const_copies = [pltpu.make_async_copy(h, v, const_sem.at[i]) for i, (h, v) in enumerate(consts)]
    for cp in const_copies:
        cp.start()

    bar = pltpu.get_barrier_semaphore()
    line = [(dx, dc) for dx in range(4) for dc in range(2) if (dx, dc) != (0, 0)]
    partners = [me.dev(dx=dx, dc=dc) for dx, dc in line]
    partners += [me.dev(dy=1), me.dev(dy=-1), me.dev(dz=1), me.dev(dz=-1)]
    for d in partners:
        pl.semaphore_signal(bar, inc=1, device_id=d, device_id_type=MESH)
    sibling = me.dev(dc=1)

    def to_sibling(i, src, dst):
        return pltpu.make_async_remote_copy(
            src_ref=src, dst_ref=dst, send_sem=pair_send.at[i], recv_sem=pair_recv.at[i],
            device_id=sibling, device_id_type=MESH)

    def lane_place():
        r = lax.broadcasted_iota(jnp.int32, (128, HALF), 0)
        m = lax.broadcasted_iota(jnp.int32, (128, HALF), 1)
        small = (r < 6) & (m == r + 6 * s_me)
        wide = (r >= 8) & (r < 32) & (m == r - 8 + 128 + 24 * x)
        return jnp.where(small | wide, 1.0, 0.0).astype(BF16)

    def line_copies(l, bufs, into, bufu, intou, sems):
        out = []
        for dx, dc in line:
            t = (c + dc) % 2
            s_to = ((x + dx) % 4) * 2 + t
            out.append(pltpu.make_async_remote_copy(
                src_ref=bufs(s_to, t), dst_ref=into.at[l, s_me], send_sem=sems.at[0], recv_sem=sems.at[1],
                device_id=me.dev(dx=dx, dc=dc), device_id_type=MESH))
        for dx in range(1, 4):
            out.append(pltpu.make_async_remote_copy(
                src_ref=bufu((x + dx) % 4), dst_ref=intou.at[l, x], send_sem=sems.at[2],
                recv_sem=sems.at[3], device_id=me.dev(dx=dx), device_id_type=MESH))
        for cp in out:
            cp.start()

    def line_wait(sems):
        seven, three = W.at[0, 0, 0, pl.ds(0, 7 * CHUNK)], W.at[0, 0, 0, pl.ds(0, 144)]
        for i, ref in enumerate((seven, seven, three, three)):
            pltpu.make_async_copy(ref, ref, sems.at[i]).wait()

    h1[0:2 * CHUNK, :] = jnp.zeros((2 * CHUNK, D), F32)
    for l in range(2):
        h1[7 * l:7 * l + 2, 0:6] = w_gain[l].astype(F32)
        h1[7 * l + 2:7 * l + 4, 0:6] = w_nbias[l].astype(F32)
        for k, ref in ((4, w_qb), (5, w_ob), (6, w_db)):
            h1[7 * l + k:7 * l + k + 1, 0:6] = ref[...].astype(F32)[l:l + 1]
    h1[0:2, 8:32] = w_ub[...].astype(F32)
    h1[16:22, 0:128] = w_kv[...].astype(F32)
    for i in range(6):
        q2, o2, d2 = w_q[i].astype(F32), w_o[i].astype(F32), w_down[i].astype(F32)
        for l in range(2):
            at = CHUNK * l
            h1[at + 22 + i:at + 23 + i, :] = q2[l:l + 1]
            h1[at + 28 + i:at + 29 + i, :] = o2[l:l + 1]
            for g in range(4):
                h1[at + 34 + 4 * i + g:at + 35 + 4 * i + g, :] = d2[l:l + 1, g * D:(g + 1) * D]
    for l in range(2):
        u = w_up[l].astype(F32)
        rawu[l] = jnp.concatenate([u[:, 0:HALF], u[:, HALF:]], axis=0).astype(BF16)

    const_copies[0].wait()
    place = lane_place()

    def prepare(l):
        vf = h1[CHUNK * l:CHUNK * l + CHUNK, :]
        v = vf.astype(BF16)
        vp = nn(v, c_perm[...]).astype(BF16).astype(F32)
        row = lax.broadcasted_iota(jnp.int32, (CHUNK, HALF), 0)
        lane = lax.broadcasted_iota(jnp.int32, (CHUNK, HALF), 1)
        if l == 0:
            head = jnp.where(row < 16, nn(v[:, 0:128], place), jnp.where(lane < 128, vf[:, 0:HALF], 0.0))
        for t in range(2):
            part = jnp.where(row < 34, vf[:, t * HALF:(t + 1) * HALF], vp[:, t * HALF:(t + 1) * HALF])
            if l == 0:
                ours = jnp.where((lane < 128) | (c == t), head, 0.0)
                part = jnp.where(row < 22, ours, part)
            chunk[l, t] = part.astype(BF16)

    def send_chunks(l):
        line_copies(l, lambda s, t: chunk.at[l, t], got, lambda xx: rawu.at[l], gotu, line_sem.at[l])
        got[l, s_me] = chunk[l, c]
        gotu[l, x] = rawu[l]

    prepare(0)
    seg2[c] = jnp.broadcast_to(seg[...], (8, TOK))
    own = pl.ds(pl.multiple_of(c * TOK, TOK), TOK)

    pl.semaphore_wait(bar, len(partners))

    def to_sibling(i, src, dst):
        return pltpu.make_async_remote_copy(
            src_ref=src, dst_ref=dst, send_sem=pair_send.at[i], recv_sem=pair_recv.at[i],
            device_id=sibling, device_id_type=MESH)

    send_chunks(0)
    seg_copy = to_sibling(0, seg2.at[c], seg2.at[c])
    seg_copy.start()
    x_copy = to_sibling(1, xin, X2.at[c])
    x_copy.start()
    c_copy = to_sibling(2, cot, gl.at[own])
    c_copy.start()
    X2[c] = xin[...]
    gl[own, :] = cot[...]
    prepare(1)
    send_chunks(1)

    half_width = HD // 8
    frequency = np.float32(rotary_base) ** (-(np.arange(half_width, dtype=np.float32) * 2.0) / (2 * half_width))
    row = lax.broadcasted_iota(jnp.int32, (half_width, TOK), 0)
    freq = jnp.zeros((half_width, TOK), F32)
    for f in range(half_width):
        freq = jnp.where(row == f, float(frequency[f]), freq)
    seg_copy.wait()
    for b in range(2):
        docs = seg2[b].astype(F32)
        over_lanes = jnp.broadcast_to(docs[0:1], (TOK, TOK))
        over_rows = over_lanes.T
        earlier = jnp.sum(jnp.where(over_rows < over_lanes, 1.0, 0.0), axis=0, keepdims=True)
        place = lax.broadcasted_iota(jnp.int32, (1, TOK), 1).astype(F32) - earlier
        angle = jnp.broadcast_to(place, (8, TOK)) * freq
        cosT[:, b * TOK:(b + 1) * TOK] = jnp.cos(angle)
        sinT[:, b * TOK:(b + 1) * TOK] = jnp.sin(angle)
        kk = lax.broadcasted_iota(jnp.int32, (TOK, TOK), 0)
        qq = lax.broadcasted_iota(jnp.int32, (TOK, TOK), 1)
        mbias[b] = jnp.where((over_rows == over_lanes) & (kk <= qq), 0.0, masked_score)
    x_copy.wait()
    c_copy.wait()

    CH = 64

    def norm_of(h):
        centred = h - jnp.mean(h, axis=-1, keepdims=True)
        inverse = lax.rsqrt(jnp.mean(centred * centred, axis=-1, keepdims=True) + norm_epsilon)
        return centred * inverse, inverse

    def normalise(i, h):
        rows = pl.ds(pl.multiple_of(i * CH, CH), CH)
        n, inverse = norm_of(h)
        n_[rows, :] = n
        r_[rows, :] = jnp.broadcast_to(inverse, (CH, 128))

    def input_rows(i):
        return X2[i // 4, pl.ds(pl.multiple_of((i % 4) * CH, CH), CH), :].astype(F32)

    @pl.loop(0, 8)
    def _(i):
        normalise(i, input_rows(i))

    for cp in const_copies[1:]:
        cp.wait()

    def quarter(k):
        return pl.multiple_of(D0 + 48 * k, 16)

    def assemble(l):
        line_wait(line_sem.at[l])
        stack = got[l].reshape(512, HALF)
        W[l, z, y, Q0:D0, :] = nn(c_qod[0:96, :], stack).astype(BF16)
        down = nn(c_qod[pl.ds(pl.multiple_of(96 + 48 * x, 16), 48), :], stack).astype(BF16)
        W[l, z, y, pl.ds(quarter(x), 48), :] = down
        if l == 0:
            kv = nn(c_kv[...], stack[:, 0:128]).astype(BF16)
            W[0, z, y, KV0:KV0 + 16, :] = jnp.concatenate([kv[0:16], kv[16:32], kv[32:48]], axis=1)
            vec = got[0, 0, 0:16, :].astype(F32)
            for s in range(1, 8):
                vec = vec + got[0, s, 0:16, :].astype(F32)
            W[0, z, y, VEC0:VEC0 + 16, :] = vec.astype(BF16)
        W[l, z, y, U0:ROWS, :] = nn(c_up[...], gotu[l].reshape(192, HALF)).astype(BF16)

    def many(n, wide):
        if wide:
            return lambda count: W.at[0, pl.ds(0, count), :, pl.ds(0, n), :]
        return lambda count: W.at[0, 0, pl.ds(0, count), pl.ds(0, n), :]

    def cut(row0, n, h):
        first = halves(n)[0]
        return pl.ds(row0 if h == 0 else pl.multiple_of(row0 + first, 16), first if h == 0 else n - first)

    def halves(n):
        first = (n + 31) // 32 * 16
        return (first, n - first)

    def gathers(l):
        g = {}

        def y_then_z(i, name, row0, n):
            g[name + "2"] = Gather(me, "y", lambda k, h: W.at[l, z, k, cut(row0, n, h), :], ag_sem.at[l, i], many(n, False))
            g[name + "3"] = Gather(me, "z", lambda k, h: W.at[l, k, pl.ds(2 * h, 2), pl.ds(row0, n), :], ag_sem.at[l, i + 1],
                                   many(n, True))

        def z_then_y(i, name, row0, n):
            g[name + "2"] = Gather(me, "z", lambda k, h: W.at[l, k, y, cut(row0, n, h), :], ag_sem.at[l, i], many(n, False))
            g[name + "3"] = Gather(me, "y", lambda k, h: W.at[l, pl.ds(2 * h, 2), k, pl.ds(row0, n), :], ag_sem.at[l, i + 1],
                                   many(n, True))

        e0 = 0 if l == 0 else Q0
        en = (D0 - e0) // 2
        y_then_z(0, "E", e0, en)
        z_then_y(2, "F", e0 + en, en)
        z_then_y(4, "D", quarter(x), 48)
        y_then_z(6, "U", U0, 112)
        z_then_y(8, "V", U0 + 112, 80)
        for i, dy in enumerate((0, 1, 3, 2)):
            g["D4", i] = Gather(me, "x", lambda k, h, dy=dy: W.at[l, pl.ds(2 * h, 2), (y + dy) % 4, pl.ds(quarter(k), 48), :],
                                ag_sem.at[l, 10 + i], many(48, True))
        return g

    g0, g1 = gathers(0), gathers(1)

    def second_stage(l, g):
        assemble(l)
        for n in "EFDUV":
            g[n + "2"].start()

    def third_stage(g):
        for n in "EFDUV":
            g[n + "2"].forward()
        for n in "EFD":
            g[n + "2"].finish()
            g[n + "3"].start()
        g["D4", 0].start()
        for n in "UV":
            g[n + "2"].finish()
        g["E3"].forward()
        g["F3"].forward()
        for n in "UV":
            g[n + "3"].start()

    def fourth_stage(g):
        g["D3"].forward()
        g["D4", 0].forward()
        g["D3"].near()
        g["D4", 1].start()
        g["D4", 2].start()
        g["U3"].forward()
        g["V3"].forward()

    def heads_ready(g):
        g["E3"].finish()
        g["F3"].finish()

    def last_quarter(g):
        g["D3"].far()
        g["D4", 3].start()
        g["D4", 1].forward()
        g["D4", 2].forward()

    def hidden_ready(g):
        g["U3"].finish()
        g["V3"].finish()

    def down_ready(g):
        g["D3"].sent()
        for i in range(4):
            g["D4", i].finish()

    second_stage(0, g0)
    third_stage(g0)
    second_stage(1, g1)
    heads_ready(g0)

    tile = W[0, :, :, VEC0:VEC0 + 16, :].reshape(256, HALF)
    wide = nn(tile[:, 0:128], c_s48[...])
    at = lax.broadcasted_iota(jnp.int32, (16, D), 1)
    total = jnp.zeros((16, D), F32)
    for m in range(16):
        total = total + jnp.where((at >= 48 * m) & (at < 48 * m + 48), wide[16 * m:16 * m + 16], 0.0)
    vecs[...] = total
    wide = nn(tile[:, 128:256], c_s96[...])
    at = lax.broadcasted_iota(jnp.int32, (16, 1536), 1)
    total = jnp.zeros((16, 1536), F32)
    for m in range(16):
        total = total + jnp.where((at >= 96 * m) & (at < 96 * m + 96), wide[16 * m:16 * m + 16], 0.0)
    for l in range(2):
        for k in range(4):
            ubv[l, k] = jnp.broadcast_to(total[l:l + 1, k * HALF:(k + 1) * HALF], (8, HALF))

    def vec(l, k):
        return vecs[7 * l + k:7 * l + k + 1, :]

    def norm_inputs(l, again=False):
        @pl.loop(0, 8)
        def _(i):
            rows = pl.ds(pl.multiple_of(i * CH, CH), CH)
            n = norm_of(input_rows(i))[0] if again else n_[rows, :]
            attn[rows, :] = (n * vec(l, 0) + vec(l, 2)).astype(BF16)
            mlp[rows, :] = (n * vec(l, 1) + vec(l, 3)).astype(BF16)

    def key_weight():
        kvw = W[0, :, :, KV0:KV0 + 16, :]
        return jnp.concatenate([kvw[..., 0:128], kvw[..., 128:256], kvw[..., 256:384]], axis=2).reshape(D, 128)

    def weight(l, row0, n=48):
        return W[l, :, :, pl.ds(row0, n), :].reshape(16 * n, HALF)

    def up_weight(l, k, h):
        return W[l, k, :, U0 + 96 * h:U0 + 96 * h + 96, :].reshape(HALF, HALF)

    def down_weight(l, k):
        return weight(l, pl.multiple_of(D0 + 48 * k, 16))

    def rotate_heads(v, heads):
        v = v.reshape(heads, HD, 512)
        cs, sn = cosT[...][None], sinT[...][None]
        u1, u2 = v[:, 0:8, :], v[:, 8:16, :]
        return jnp.concatenate([u1 * cs - u2 * sn, u2 * cs + u1 * sn, v[:, 16:, :]], axis=1).reshape(heads * HD, 512)

    def rotate_heads_back(v, heads):
        v = v.reshape(heads, HD, 512)
        cs, sn = cosT[...][None], sinT[...][None]
        u1, u2 = v[:, 0:8, :], v[:, 8:16, :]
        return jnp.concatenate([u1 * cs + u2 * sn, u2 * cs - u1 * sn, v[:, 16:, :]], axis=1).reshape(heads * HD, 512)

    def serve(i, points):
        for at, step in points.items():
            pl.when(i == at)(step)

    def steps(*todo):
        def run():
            for step, *args in todo:
                step(*args)

        return run

    def down_block(l, rows):
        acc[rows, :] = nt(mixed[l, rows, :], weight(l, O0))
        for k in range(4):
            acc[rows, :] += nt(act[l, k, rows, :], down_weight(l, k))

    def forward(l, in_heads, before_ffn, in_ffn):
        norm_inputs(l)
        if l == 0:
            kv = nn(attn[...], key_weight()).T
            keys = rotate_heads(kv[0:HD], 1)
            kvT[0:HD, :] = keys.astype(BF16)
            kvT[HD:, :] = kv[HD:].astype(BF16)
            k_[...] = keys.T.astype(BF16)
            v_[...] = kv[HD:].T.astype(BF16)
        qb = vec(l, 4)
        qb = jnp.where(c == 0, qb[:, 0:HALF], qb[:, HALF:])
        q = nn(attn[...], weight(l, Q0)) + qb
        qT[l] = rotate_heads(q.T, 6).astype(BF16)

        @pl.loop(0, 12)
        def _(i):
            serve(i, in_heads)
            h, b = i // 2, i % 2
            hs = pl.ds(pl.multiple_of(h * HD, HD), HD)
            bs = pl.ds(pl.multiple_of(b * TOK, TOK), TOK)
            s = nn(k_[bs, :], qT[l, hs, bs]) * scale + mbias[b]
            e = jnp.exp(s - jnp.max(s, axis=0, keepdims=True))
            low = (e * (1.0 / jnp.sum(e, axis=0, keepdims=True))).astype(BF16)
            p_[l, h, b] = low
            mixT[hs, bs] = nn(kvT[HD:, bs], low).astype(BF16)

        mixed[l] = mixT[...].T
        before_ffn()

        @pl.loop(0, 4)
        def _(k):
            serve(k, in_ffn)
            for b in range(2):
                rows = slice(b * TOK, (b + 1) * TOK)
                hid = nt(mlp[rows, 0:HALF], up_weight(l, k, 0)) + nt(mlp[rows, HALF:], up_weight(l, k, 1))
                hid = hid + ubv[l, k, 0:1, :]
                phi = 0.5 * (1.0 + lax.erf(hid * root_half))
                low = (hid * phi).astype(BF16)
                act[l, k, rows, :] = low
                slope[l, k, rows, :] = (phi + hid * jnp.exp(-0.5 * hid * hid) * inverse_root_tau).astype(BF16)

    forward(
        0,
        {0: steps((fourth_stage, g0)), 3: steps((third_stage, g1)), 5: steps((last_quarter, g0)), 9: steps((g0["D4", 3].forward,))},
        steps((hidden_ready, g0)),
        {},
    )
    down_ready(g0)
    swap = [to_sibling(3 + b, xs.at[b], xr.at[b]) for b in range(2)]
    for b in range(2):
        down_block(0, slice(b * TOK, (b + 1) * TOK))
        xs[b] = acc[b * TOK:(b + 1) * TOK, :].astype(BF16)
        swap[b].start()
        if b == 0:
            fourth_stage(g1)
    heads_ready(g1)
    for cp in swap:
        cp.wait()

    @pl.loop(0, 8)
    def _(i):
        b = i // 4
        rows = pl.ds(pl.multiple_of((i % 4) * CH, CH), CH)
        h = X2[b, rows, :].astype(F32) + (vec(0, 5) + vec(0, 6))
        h = h + (xs[b, rows, :].astype(F32) + xr[b, rows, :].astype(F32))
        normalise(i, h)

        @pl.when(b == c)
        def _():
            h1[rows, :] = h

    forward(
        1,
        {2: steps((last_quarter, g1)), 7: steps((g1["D4", 3].forward,))},
        steps((hidden_ready, g1)),
        {},
    )
    down_ready(g1)
    other = pl.ds(pl.multiple_of((1 - c) * TOK, TOK), TOK)
    down_block(1, other)
    xs[0] = acc[other, :].astype(BF16)
    y_copy = to_sibling(5, xs.at[0], xr.at[2])
    y_copy.start()
    down_block(1, own)
    y_copy.wait()
    out_y[...] = (h1[...] + (vec(1, 5) + vec(1, 6)) + acc[own, :] + xr[2].astype(F32)).astype(BF16)

    def scatters(l):
        gslot = 2 if l == 1 else 1
        g = {}

        def z_then_y(i, n2, n3, row0, n, b2, b3):
            g[n2] = Scatter(me, "z", lambda k, h: W.at[gslot, k, pl.ds(2 * h, 2), pl.ds(row0, n), :], rs_sem.at[l, i],
                            many(n, True), b2.at[l], (2,), (n, n))
            g[n3] = Scatter(me, "y", lambda k, h: W.at[gslot, z, k, cut(row0, n, h), :], rs_sem.at[l, i + 1],
                            many(n, False), b3.at[l], (), halves(n))

        def y_then_z(i, n2, n3, row0, n, b2, b3):
            g[n2] = Scatter(me, "y", lambda k, h: W.at[gslot, pl.ds(2 * h, 2), k, pl.ds(row0, n), :], rs_sem.at[l, i],
                            many(n, True), b2.at[l], (2,), (n, n))
            g[n3] = Scatter(me, "z", lambda k, h: W.at[gslot, k, y, cut(row0, n, h), :], rs_sem.at[l, i + 1],
                            many(n, False), b3.at[l], (), halves(n))

        for i, dz in enumerate((2, 1, 3, 0)):
            g["D1", i] = Scatter(me, "x", lambda k, h, dz=dz: W.at[gslot, (z + dz) % 4, pl.ds(2 * h, 2), pl.ds(quarter(k), 48), :],
                                 rs_sem.at[l, i], many(48, True), bD1.at[l, i], (2,), (48, 48))
        z_then_y(4, "D2", "D3", quarter(x), 48, bD2, bD3)
        y_then_z(6, "O2", "O3", O0, 48, bO2, bO3)
        z_then_y(8, "U2", "U3", U0, 96, bU2, bU3)
        y_then_z(14, "V2", "V3", U0 + 96, 96, bV2, bV3)
        a0 = 0 if l == 0 else VEC0
        z_then_y(10, "A2", "A3", a0, 48 - a0, bA2, bA3)
        y_then_z(12, "B2", "B3", 48, 32, bB2, bB3)
        return g

    def finish_line(l):
        gslot = 2 if l == 1 else 1
        B = W.at[gslot, z, y]
        rowd = lax.broadcasted_iota(jnp.int32, (288, HALF), 0)
        lo = 96 + 48 * x
        blk = B[Q0:U0, :].astype(F32)
        blk = jnp.where((rowd < 96) | ((rowd >= lo) & (rowd < lo + 48)), blk, 0.0).astype(BF16)
        stack = nn(c_qodT[...], blk)
        if l == 0:
            kv = B[KV0:KV0 + 16, :]
            kv = jnp.concatenate([kv[:, 0:128], kv[:, 128:256], kv[:, 256:384]], axis=0)
            stack = stack + jnp.concatenate([nn(c_kvT[...], kv), jnp.zeros((512, 256), F32)], axis=1)
        stack = stack.astype(BF16).reshape(8, CHUNK, HALF)
        got[l] = stack
        for s in range(8):
            got[l, s, 0:16, :] = B[VEC0:VEC0 + 16, :]
        gotu[l] = nn(c_upT[...], B[U0:ROWS, :]).astype(BF16).reshape(4, 48, HALF)
        line_copies(l, lambda s, t: got.at[l, s], rgot, lambda xx: gotu.at[l, xx], rgotu, line_sem.at[2 + l])
        rgot[l, s_me] = got[l, s_me]
        rgotu[l, x] = gotu[l, x]

    def last_sums(l):
        line_wait(line_sem.at[2 + l])
        halves = []
        for t in range(2):
            v = rgot[l, t].astype(F32)
            for xx in range(1, 4):
                v = v + rgot[l, 2 * xx + t].astype(F32)
            halves.append(v)
        v = jnp.concatenate(halves, axis=1)
        hi = v.astype(BF16)
        lo = (v - hi.astype(F32)).astype(BF16)
        unperm = nt(hi, c_perm[...]) + nt(lo, c_perm[...])
        row = lax.broadcasted_iota(jnp.int32, (CHUNK, HALF), 0)
        lane = lax.broadcasted_iota(jnp.int32, (CHUNK, HALF), 1)
        both = halves[0] + halves[1]
        mine = jnp.where(lane < 128, both, jnp.where(c == 0, halves[0], halves[1]))
        hi = mine.astype(BF16)
        lo = (mine - hi.astype(F32)).astype(BF16)
        lp = lane_place()
        small = nt(hi, lp) + nt(lo, lp)
        first = jnp.where(row < 34, halves[0], unperm[:, 0:HALF])
        first = jnp.where(row < 22, both, first)
        out_v[l, :, 0:HALF] = first
        out_v[l, :, HALF:] = jnp.where(row < 34, halves[1], unperm[:, HALF:])
        out_v[l, 0:16, 0:128] = small[0:16]
        u = rgotu[l, 0].astype(F32)
        for xx in range(1, 4):
            u = u + rgotu[l, xx].astype(F32)
        out_u[l] = u

    r1, r0 = scatters(1), scatters(0)

    def first_sums(r):
        for i in range(4):
            r["D1", i].start()
        r["O2"].start()

    def forward_on(r, *names):
        for n in names:
            r[n].forward()

    def next_ring(r, *names):
        for n in names:
            r[n + "2"].finish()
            r[n + "3"].start()

    def down_second(r):
        r["D1", 0].finish()
        r["D2"].start_far()
        r["D1", 1].finish()
        r["D1", 2].finish()
        r["D2"].start_near()
        r["D1", 3].finish()

    def finish_third(r, names):
        for n in names:
            r[n].finish()

    def backward(l, r, after_norm, after_down, in_ffn, before_heads, in_heads, before_query):
        gslot = 2 if l == 1 else 1
        G = W.at[gslot]
        after_norm()
        glT[...] = gl[...].T
        vg[5:6, :] = jnp.sum(gl[own, :].astype(F32), axis=0, keepdims=True)

        for b in range(2):
            rows = slice(b * HALF, (b + 1) * HALF)
            part = nn(glT[rows, :], mixed[l]).astype(BF16).reshape(2, 4, 48, HALF)
            G[2 * b:2 * b + 2, :, O0:O0 + 48, :] = part

        acc[...] = jnp.zeros_like(acc)

        @pl.loop(0, 4)
        def _(k):
            rows_d = pl.ds(pl.multiple_of(D0 + 48 * k, 16), 48)
            for b in range(2):
                rows = slice(b * HALF, (b + 1) * HALF)
                part = nn(glT[rows, :], act[l, k]).astype(BF16).reshape(2, 4, 48, HALF)
                G[2 * b:2 * b + 2, :, rows_d, :] = part

        first_sums(r)
        after_down()

        @pl.loop(0, 4)
        def _(k):
            serve(k, in_ffn)
            sums = jnp.zeros((1, HALF), F32)
            for b in range(2):
                rows = slice(b * TOK, (b + 1) * TOK)
                gh = nn(gl[rows, :], down_weight(l, k)) * slope[l, k, rows, :].astype(F32)
                gh = gh.astype(BF16)
                slope[l, k, rows, :] = gh
                sums = sums + jnp.sum(gh.astype(F32), axis=0, keepdims=True)
                for h in range(2):
                    acc[rows, h * HALF:(h + 1) * HALF] += nn(gh, up_weight(l, k, h))
            ubg[k] = jnp.broadcast_to(sums, (8, HALF))
            ghT = slope[l, k].T
            for h in range(2):
                part = nn(ghT, mlp[:, h * HALF:(h + 1) * HALF]).astype(BF16).reshape(4, 96, HALF)
                G[k, :, U0 + 96 * h:U0 + 96 * h + 96, :] = part

        r["U2"].start()
        r["V2"].start()
        before_heads()

        for b in range(2):
            rows = slice(b * TOK, (b + 1) * TOK)
            gm[rows, :] = nn(gl[rows, :], weight(l, O0)).astype(BF16)
        gmT[...] = gm[...].T

        if l == 1:
            dk[...] = jnp.zeros_like(dk)
            dv[...] = jnp.zeros_like(dv)

        @pl.loop(0, 12)
        def _(i):
            h, b = i // 2, i % 2
            hs = pl.ds(pl.multiple_of(h * HD, HD), HD)
            bs = pl.ds(pl.multiple_of(b * TOK, TOK), TOK)
            serve(i, in_heads)
            low = p_[l, h, b]
            probs = low.astype(F32)
            t = probs * nn(v_[bs, :], gmT[hs, bs])
            grad = (t - probs * jnp.sum(t, axis=0, keepdims=True)).astype(BF16)
            dq = nn(kvT[0:HD, bs], grad) * scale
            cs, sn = cosT[:, bs], sinT[:, bs]
            u1, u2 = dq[0:8], dq[8:16]
            dq = jnp.concatenate([u1 * cs + u2 * sn, u2 * cs - u1 * sn, dq[16:]], axis=0)
            mixT[hs, bs] = dq.astype(BF16)
            dk[bs, :] += nt(grad, qT[l, hs, bs])
            dv[bs, :] += nt(low, gmT[hs, bs])

        before_query()
        low = mixT[...].T
        gm[...] = low
        qsum = jnp.sum(low.astype(F32), axis=0, keepdims=True)
        zero = jnp.zeros_like(qsum)
        vg[4:5, :] = jnp.concatenate([jnp.where(c == 0, qsum, zero), jnp.where(c == 0, zero, qsum)], axis=1)
        if l == 0:
            keys = rotate_heads_back((dk[...] * scale).T, 1).T
            gs[...] = jnp.concatenate([keys, dv[...]], axis=1).astype(BF16)

    def query_grad(l, r):
        G = W.at[2 if l == 1 else 1]
        for b in range(2):
            rows = slice(b * HALF, (b + 1) * HALF)
            part = nn(attnT[rows, :], gm[...]).astype(BF16).reshape(2, 4, 48, HALF)
            G[2 * b:2 * b + 2, :, Q0:Q0 + 48, :] = part
        r["B2"].start()
        if l == 0:
            dkv = nn(attnT[...], gs[...]).astype(BF16).reshape(4, 4, 48, 128)
            G[:, :, KV0:KV0 + 16, :] = jnp.concatenate([dkv[:, :, 0:16], dkv[:, :, 16:32], dkv[:, :, 32:48]], axis=3)

    def fold_block(l, b, sums):
        rows = slice(b * TOK, (b + 1) * TOK)
        ea = nt(gm[rows, :], weight(l, Q0))
        if l == 0:
            ea = ea + nt(gs[rows, :], key_weight())
        h1[...] = ea

        def fold(i, sums):
            rows = pl.ds(pl.multiple_of(i * CH, CH), CH)
            all_rows = pl.ds(pl.multiple_of(b * TOK + i * CH, CH), CH)
            n = n_[all_rows, :] if l == 1 else norm_of(X2[b, rows, :].astype(F32))[0]
            ea, em = h1[rows, :], acc[all_rows, :]
            xs[b, rows, :] = (ea * vec(l, 0) + em * vec(l, 1)).astype(BF16)
            add = [ea * n, em * n, ea, em]
            return tuple(s + jnp.sum(a, axis=0, keepdims=True) for s, a in zip(sums, add))

        return lax.fori_loop(0, 4, fold, sums)

    def vector_grad(l, r, sums):
        G = W.at[2 if l == 1 else 1]
        for k in range(4):
            vg[k:k + 1, :] = sums[k]
        at = lax.broadcasted_iota(jnp.int32, (16, D), 1)
        rowk = lax.broadcasted_iota(jnp.int32, (16, D), 0)
        vv = jnp.where(rowk < 6, vg[...], 0.0)
        parts = [jnp.where((at >= 48 * m) & (at < 48 * m + 48), vv, 0.0).astype(BF16) for m in range(16)]
        small = nt(jnp.concatenate(parts, axis=0), c_s48[...]).astype(BF16)
        ub = jnp.concatenate([ubg[k][0:1, :] for k in range(4)], axis=1)
        at = lax.broadcasted_iota(jnp.int32, (16, 1536), 1)
        rowk = lax.broadcasted_iota(jnp.int32, (16, 1536), 0)
        ub = jnp.where(rowk == 6, jnp.broadcast_to(ub, (16, 1536)), 0.0)
        parts = [jnp.where((at >= 96 * m) & (at < 96 * m + 96), ub, 0.0).astype(BF16) for m in range(16)]
        wide = nt(jnp.concatenate(parts, axis=0), c_s96[...]).astype(BF16)
        both = jnp.concatenate([small, wide, jnp.zeros((256, 128), BF16)], axis=1)
        G[:, :, VEC0:VEC0 + 16, :] = both.reshape(4, 4, 16, HALF)
        r["A2"].start()

    def through_norm(n, inverse, g, s):
        m1 = jnp.mean(s, axis=-1, keepdims=True)
        m2 = jnp.mean(s * n, axis=-1, keepdims=True)
        return g + inverse * (s - m1 - n * m2)

    no_sums = (jnp.zeros((1, D), F32),) * 4

    attnT[...] = attn[...].T
    backward(
        1, r1, steps(), steps(),
        {3: steps((forward_on, r1, ("D1", 0), "O2"))},
        steps((forward_on, r1, ("D1", 1))),
        {4: steps((next_ring, r1, "O"), (forward_on, r1, ("D1", 2))), 9: steps((forward_on, r1, ("D1", 3)))},
        steps((forward_on, r1, "U2", "V2", "O3")),
    )
    swap = [to_sibling(6 + b, xs.at[b], xr.at[b]) for b in range(2)]
    sums = no_sums
    for b in range(2):
        sums = fold_block(1, b, sums)
        swap[b].start()
    query_grad(1, r1)
    vector_grad(1, r1, sums)
    r1["O3"].finish()
    norm_inputs(0, again=True)
    attnT[...] = attn[...].T
    down_second(r1)
    for cp in swap:
        cp.wait()

    @pl.loop(0, 8)
    def _(i):
        b = i // 4
        rows = pl.ds(pl.multiple_of((i % 4) * CH, CH), CH)
        s = xs[b, rows, :].astype(F32) + xr[b, rows, :].astype(F32)
        all_rows = pl.ds(pl.multiple_of(i * CH, CH), CH)
        g = through_norm(n_[all_rows, :], r_[all_rows, 0:1], gl[all_rows, :].astype(F32), s)
        gl[all_rows, :] = g.astype(BF16)

        @pl.when(b == c)
        def _():
            g_[rows, :] = g

    backward(
        0, r0,
        steps((forward_on, r1, "A2", "B2")),
        steps((forward_on, r1, "D2")),
        {
            1: steps((next_ring, r1, "U", "V")),
            2: steps((next_ring, r1, "A", "B", "D")),
            3: steps((forward_on, r1, "U3", "V3")),
        },
        steps((forward_on, r0, ("D1", 0), "O2"), (forward_on, r1, "A3", "B3", "D3")),
        {
            3: steps((forward_on, r0, ("D1", 1))),
            6: steps((forward_on, r0, ("D1", 2)), (next_ring, r0, "O")),
            10: steps((forward_on, r0, ("D1", 3))),
        },
        steps((forward_on, r0, "U2", "V2", "O3")),
    )
    query_grad(0, r0)
    sums = no_sums
    for b in range(2):
        sums = fold_block(0, b, sums)
    swap = to_sibling(8, xs.at[1 - c], xr.at[2])
    swap.start()
    vector_grad(0, r0, sums)
    finish_third(r1, ("U3", "V3", "A3", "B3", "D3"))
    finish_line(1)
    swap.wait()

    @pl.loop(0, 4)
    def _(i):
        rows = pl.ds(pl.multiple_of(i * CH, CH), CH)
        s = xs[c, rows, :].astype(F32) + xr[2, rows, :].astype(F32)
        n, inverse = norm_of(X2[c, rows, :].astype(F32))
        out_gx[rows, :] = through_norm(n, inverse, g_[rows, :], s).astype(BF16)

    forward_on(r0, "B2", "A2")
    down_second(r0)
    next_ring(r0, "U", "V", "B", "A")
    forward_on(r0, "D2", "U3", "V3")
    next_ring(r0, "D")
    forward_on(r0, "B3", "A3", "D3")
    last_sums(1)
    finish_third(r0, ("O3", "U3", "V3", "A3", "B3", "D3"))
    finish_line(0)
    last_sums(0)


def vmem(*shape, dtype=BF16):
    return pltpu.VMEM(shape, dtype)


def make_call():
    T2 = 2 * TOK
    scratch = [
        vmem(3, 4, 4, ROWS, HALF), vmem(2, 2, CHUNK, HALF), vmem(2, 48, HALF), vmem(2, 8, CHUNK, HALF), vmem(2, 4, 48, HALF),
        vmem(16, D, dtype=F32), vmem(2, 4, 8, HALF, dtype=F32),
        vmem(2, TOK, D), vmem(T2, D), vmem(2, 8, TOK, dtype=jnp.int32), vmem(8, T2, dtype=F32), vmem(8, T2, dtype=F32),
        vmem(2, TOK, TOK, dtype=F32), vmem(T2, D, dtype=F32), vmem(T2, 128, dtype=F32), vmem(TOK, D, dtype=F32),
        vmem(T2, D), vmem(T2, D), vmem(128, T2), vmem(T2, HD), vmem(T2, HD), vmem(2, HALF, T2), vmem(2, 6, 2, TOK, TOK),
        vmem(HALF, T2), vmem(2, T2, HALF), vmem(2, 4, T2, HALF), vmem(2, 4, T2, HALF),
        vmem(T2, D, dtype=F32), vmem(D, T2), vmem(D, T2), vmem(T2, HALF), vmem(HALF, T2),
        vmem(T2, HD, dtype=F32), vmem(T2, HD, dtype=F32), vmem(T2, 128), vmem(16, D, dtype=F32),
        vmem(4, 8, HALF, dtype=F32), vmem(TOK, D, dtype=F32), vmem(2, TOK, D), vmem(3, TOK, D),
        vmem(2, 6, 2, 48, HALF), vmem(2, 6, 2, 32, HALF), vmem(2, 6, 2, 48, HALF), vmem(2, 6, 2, 96, HALF), vmem(2, 6, 2, 96, HALF),
        vmem(2, 4, 6, 2, 48, HALF), vmem(2, 6, 2, 48, HALF),
        vmem(2, 6, 32, HALF), vmem(2, 6, 16, HALF), vmem(2, 6, 32, HALF), vmem(2, 6, 48, HALF), vmem(2, 6, 48, HALF), vmem(2, 6, 32, HALF),
        vmem(2, 8, CHUNK, HALF), vmem(2, 4, 48, HALF),
        *[vmem(*v.shape) for v in (CONSTS[i] for i in range(9))],
        pltpu.SemaphoreType.DMA((9,)), pltpu.SemaphoreType.DMA((9,)), pltpu.SemaphoreType.DMA((9,)),
        pltpu.SemaphoreType.DMA((4, 4)), pltpu.SemaphoreType.DMA((2, 14, 5)), pltpu.SemaphoreType.DMA((2, 16, 4)),
    ]
    whole = pl.BlockSpec(memory_space=pltpu.VMEM)
    return pl.pallas_call(
        kernel,
        out_shape=(
            jax.ShapeDtypeStruct((TOK, D), BF16),
            jax.ShapeDtypeStruct((TOK, D), BF16),
            jax.ShapeDtypeStruct((2, CHUNK, D), F32),
            jax.ShapeDtypeStruct((2, 48, HALF), F32),
        ),
        in_specs=[whole] * 14 + [pl.BlockSpec(memory_space=pl.ANY)] * 9,
        out_specs=(whole,) * 4,
        scratch_shapes=scratch,
        compiler_params=pltpu.CompilerParams(
            collective_id=0, has_side_effects=True, vmem_limit_bytes=64 * 2**20 - 65536
        ),
        name="two_layers",
    )


def pack_kernel(
    y, gx, v, u,
    o_y, o_gx, o_gain, o_nbias, o_q, o_qb, o_kv, o_o, o_ob, o_up, o_ub, o_down, o_db,
):
    o_y[...] = y[...]
    o_gx[...] = gx[...]
    for l in range(2):
        o_gain[l] = v[l, 0:2, 0:6]
        o_nbias[l] = v[l, 2:4, 0:6]
        o_qb[l:l + 1, :] = v[l, 4:5, 0:6]
        o_ob[l:l + 1, :] = v[l, 5:6, 0:6]
        o_db[l:l + 1, :] = v[l, 5:6, 0:6]
        o_ub[l:l + 1, :] = v[l, 6:7, 8:32]
        for h in range(2):
            o_up[l, :, h * HALF:(h + 1) * HALF] = u[l, 24 * h:24 * h + 24, :]
        for i in range(6):
            o_q[i, l:l + 1, :] = v[l, 22 + i:23 + i, :]
            o_o[i, l:l + 1, :] = v[l, 28 + i:29 + i, :]
            for g in range(4):
                o_down[i, l:l + 1, g * D:(g + 1) * D] = v[l, 34 + 4 * i + g:35 + 4 * i + g, :]
    o_kv[...] = v[0, 16:22, 0:128]


def pack(y, gx, v, u):
    whole = pl.BlockSpec(memory_space=pltpu.VMEM)
    shapes = [(2, 2, 6), (2, 2, 6), (6, 2, D), (2, 6), (6, 128), (6, 2, D), (2, 6), (2, 24, D), (2, 24), (6, 2, FF), (2, 6)]
    return pl.pallas_call(
        pack_kernel,
        out_shape=tuple(
            [jax.ShapeDtypeStruct((TOK, D), BF16)] * 2 + [jax.ShapeDtypeStruct(shape, F32) for shape in shapes]),
        in_specs=[whole] * 4,
        out_specs=(whole,) * 13,
        name="results",
    )(y, gx, v, u)


def on_device(
    layer_input, segments, norm_gain, norm_bias, query_weight, query_bias, keyval_weight, output_weight,
    output_bias, upward_weight, upward_bias, downward_weight, downward_bias, cotangent,
):
    consts = [jnp.asarray(v, BF16) for v in CONSTS]
    y, gx, gain, nbias, q, qb, kv, o, ob, up, ub, down, db = pack(*make_call()(
        layer_input, segments, cotangent, norm_gain, norm_bias, query_weight.transpose(1, 0, 2), query_bias,
        keyval_weight, output_weight.transpose(2, 0, 1), output_bias, upward_weight.transpose(0, 2, 1), upward_bias,
        downward_weight.transpose(2, 0, 1), downward_bias, *consts))
    return (
        y, gx, gain, nbias, q.transpose(1, 0, 2), qb, kv, o.transpose(1, 2, 0), ob, up.transpose(0, 2, 1), ub,
        down.transpose(1, 2, 0), db,
    )


def solution(mesh):
    in_specs = (
        P(("dp", "fsdp"), None),
        P(("dp", "fsdp"), None),
        P(None, None, ("dp", "fsdp")),
        P(None, None, ("dp", "fsdp")),
        P(None, ("dp", "fsdp"), None),
        P(None, ("dp", "fsdp")),
        P(("dp", "fsdp"), None),
        P(None, None, ("dp", "fsdp")),
        P(None, ("dp", "fsdp")),
        P(None, None, ("dp", "fsdp")),
        P(None, ("dp", "fsdp")),
        P(None, None, ("dp", "fsdp")),
        P(None, ("dp", "fsdp")),
        P(("dp", "fsdp"), None),
    )
    out_specs = (
        P(("dp", "fsdp"), None),
        P(("dp", "fsdp"), None),
        P(None, None, ("dp", "fsdp")),
        P(None, None, ("dp", "fsdp")),
        P(None, ("dp", "fsdp"), None),
        P(None, ("dp", "fsdp")),
        P(("dp", "fsdp"), None),
        P(None, None, ("dp", "fsdp")),
        P(None, ("dp", "fsdp")),
        P(None, None, ("dp", "fsdp")),
        P(None, ("dp", "fsdp")),
        P(None, None, ("dp", "fsdp")),
        P(None, ("dp", "fsdp")),
    )
    return jax.shard_map(on_device, mesh=mesh, in_specs=in_specs, out_specs=out_specs, check_vma=False)
```

time: 1880 us -> 178 us (0.09); the launches traced: 1850 us -> 177 us
  blocking collectives: 717 us -> 0 us
  starting transfers between devices: 497 us -> 0 us
  local copies, waits for them, and re-layouts: 285 us -> 0 us
  waiting for transfers between devices: 195 us -> 0 us
  Pallas kernels: 0 us -> 176 us
  matrix products: 100 us -> 0 us
  other arithmetic: 39.8 us -> 0 us
  between operations: 20.5 us -> 0.83 us
    unnamed x3 -> x0, blocking collectives: 545 us -> none
    unnamed x193 -> x0, starting transfers between devices: 496 us -> none
    unnamed x584 -> x0, local copies, waits for them, and re-layouts: 219 us -> none
    all_gather x8 -> x0, waiting for transfers between devices: 188 us -> none  [the longest x1 61.7 us: on_device(): lax.all_gather(downward_weight[1], ('dp', 'fsdp'), axis=1, tiled=True)]
    pallas_call x0 -> x2, Pallas kernels: none -> 176 us  [the longest x1 174 us: on_device(): make_call()]
    all_gather x5 -> x0, blocking collectives: 172 us -> none  [the longest x1 38.8 us: on_device(): lax.all_gather(norm_bias[1], ('dp', 'fsdp'), axis=1, tiled=True)]
    dot_general x41 -> x0, matrix products: 100 us -> none  [the longest x9 32.4 us: product(): return jnp.dot(left, right, preferred_element_type=jnp.float32)]
    all_gather x4 -> x0, local copies, waits for them, and re-layouts: 50.3 us -> none  [the longest x1 19.8 us: on_device(): lax.all_gather(downward_weight[0], ('dp', 'fsdp'), axis=1, tiled=True)]
  transfers between devices with their start and end apart: 203 -> 0, of which waited for: 6 -> 0; matrix products, arithmetic and copies ran while one was open for 43% -> 0% of each run, Pallas kernels for 0% -> 0%
where the time goes in v1:
time: 178 us; the launch traced here: 177 us
  Pallas kernels  176 us (99%)
    pallas_call x1, Pallas kernels, on_device(): make_call()  174 us

profile of v1, /device:TPU:1, one launch (start us, length us, event | category | flops | bytes accessed | tf_op | source)
XLA Modules:
  0.0 177.2 jit_solution(9644665601799921852)
XLA Ops:
  0.7 174.0 %two_layers.1 = (bf16[256,768]{1,0:T(8,128)(2,1)}, bf16[256,768]{1,0:T(8,128)(2,1)}, f32[2,64,768]{2,1,0:T(8,128)}, f32[2,48,384]{2,1,0:T(8,128)}) custom-call(bf16[256,768]{1,0:T(8,128)(2,1)} %xin.1, s32[1,256]{1,0:T(1,128)} %seg.1, bf16[256,768]{1,0:T(8,128)(2,1)} %cot.1, bf16[2,2,6]{2,1,0:T(2,128)(2,1)} %w_gain.1, bf16[2,2,6]{2,1,0:T(2,128)(2,1)} %w_nbias.1, ...), custom_call_target="tpu_custom_call" | custom-call | tf_op jit(solution)/shard_map/two_layers/pallas_call | solution.py:1070
  174.6 2.3 %results.1 = (bf16[256,768]{1,0:T(8,128)(2,1)}, bf16[256,768]{1,0:T(8,128)(2,1)}, f32[2,2,6]{2,1,0:T(2,128)}, f32[2,2,6]{2,1,0:T(2,128)}, f32[6,2,768]{2,1,0:T(2...) custom-call(bf16[256,768]{1,0:T(8,128)(2,1)} %get-tuple-element.30.y, ...), custom_call_target="tpu_custom_call" | custom-call | tf_op jit(solution)/shard_map/results/pallas_call | solution.py:1055

commit v2 on v1

--- a/solution.py
+++ b/solution.py
@@ -41,6 +41,15 @@
             for g in range(4):
                 qod[96 + 48 * g + r, s * CHUNK + 34 + 4 * i + g] = 1
             kv[r, s * CHUNK + 16 + i] = 1
+    sums = np.zeros((256, 160), np.float32)
+    sums_kv = np.zeros((256, 48), np.float32)
+    for s in range(8):
+        for i in range(6):
+            for kind in range(3):
+                sums[s * 32 + 6 * kind + i, 48 * kind + s * 6 + i] = 1
+            sums_kv[s * 32 + 18 + i, s * 6 + i] = 1
+        for k in range(8):
+            sums[s * 32 + 24 + k, 144 + k] = 1
     up = np.zeros((192, 192), np.float32)
     for h in range(2):
         for x in range(4):
@@ -55,7 +64,7 @@
     spread48[np.arange(768) % 48, np.arange(768)] = 1
     spread96 = np.zeros((128, 1536), np.float32)
     spread96[np.arange(1536) % 96, np.arange(1536)] = 1
-    return qod, kv, up, perm, spread48, spread96, qod.T, kv.T, up.T
+    return qod, kv, up, perm, spread48, spread96, sums, sums_kv, up.T
 
 
 CONSTS = place_constants()
@@ -219,14 +228,33 @@
         self.sent()
 
 
+class Direct(Ring):
+    def __init__(self, me, axis, view, sems, many, buf):
+        super().__init__(me, axis, view, sems, many)
+        self.buf = buf
+
+    def start(self):
+        for j, to in enumerate((2, 1, -1)):
+            self._copy(to, self.view((self.p + to) % 4), self.buf.at[j], 1).start()
+
+    def finish(self):
+        self._await(self.many(3), 1)
+        target = self.view(self.p)
+        total = target[...].astype(F32)
+        for j in range(3):
+            total = total + self.buf[j].astype(F32)
+        target[...] = total.astype(BF16)
+        self.sent()
+
+
 def kernel(
-    xin, seg, cot, w_gain, w_nbias, w_q, w_qb, w_kv, w_o, w_ob, w_up, w_ub, w_down, w_db, h_qod, h_kv, h_up, h_perm, h_s48, h_s96, h_qodT, h_kvT, h_upT,
+    xin, seg, cot, w_gain, w_nbias, w_q, w_qb, w_kv, w_o, w_ob, w_up, w_ub, w_down, w_db, h_qod, h_kv, h_up, h_perm, h_s48, h_s96, h_sums, h_sums_kv, h_upT,
     out_y, out_gx, out_v, out_u,
     W, chunk, rawu, got, gotu, vecs, ubv,
     X2, gl, seg2, cosT, sinT, mbias, n_, r_, h1, attn, mlp, kvT, k_, v_, qT, p_, mixT, mixed, act, slope,
     acc, glT, attnT, gm, gmT, dk, dv, gs, vg, ubg, g_, xs, xr,
-    bA2, bB2, bO2, bU2, bV2, bD1, bD2, bA3, bB3, bO3, bU3, bV3, bD3, rgot, rgotu,
-    c_qod, c_kv, c_up, c_perm, c_s48, c_s96, c_qodT, c_kvT, c_upT,
+    bA2, bB2, bO2, bU2, bD1, bD2, bA3, bB3, bO3, bU3, bD3, back, rgot, rgotu,
+    c_qod, c_kv, c_up, c_perm, c_s48, c_s96, c_sums, c_sums_kv, c_upT,
     const_sem, pair_send, pair_recv, line_sem, ag_sem, rs_sem,
 ):
     me = Place()
@@ -234,7 +262,7 @@
     s_me = x * 2 + c
 
     consts = [(h_perm, c_perm), (h_qod, c_qod), (h_kv, c_kv), (h_up, c_up), (h_s48, c_s48), (h_s96, c_s96),
-              (h_qodT, c_qodT), (h_kvT, c_kvT), (h_upT, c_upT)]
+              (h_sums, c_sums), (h_sums_kv, c_sums_kv), (h_upT, c_upT)]
     const_copies = [pltpu.make_async_copy(h, v, const_sem.at[i]) for i, (h, v) in enumerate(consts)]
     for cp in const_copies:
         cp.start()
@@ -242,7 +270,7 @@
     bar = pltpu.get_barrier_semaphore()
     line = [(dx, dc) for dx in range(4) for dc in range(2) if (dx, dc) != (0, 0)]
     partners = [me.dev(dx=dx, dc=dc) for dx, dc in line]
-    partners += [me.dev(dy=1), me.dev(dy=-1), me.dev(dz=1), me.dev(dz=-1)]
+    partners += [me.dev(dy=d) for d in (1, 2, 3)] + [me.dev(dz=d) for d in (1, 2, 3)]
     for d in partners:
         pl.semaphore_signal(bar, inc=1, device_id=d, device_id_type=MESH)
     sibling = me.dev(dc=1)
@@ -274,8 +302,8 @@
         for cp in out:
             cp.start()
 
-    def line_wait(sems):
-        seven, three = W.at[0, 0, 0, pl.ds(0, 7 * CHUNK)], W.at[0, 0, 0, pl.ds(0, 144)]
+    def line_wait(sems, rows=CHUNK):
+        seven, three = W.at[0, 0, 0, pl.ds(0, 7 * rows)], W.at[0, 0, 0, pl.ds(0, 144)]
         for i, ref in enumerate((seven, seven, three, three)):
             pltpu.make_async_copy(ref, ref, sems.at[i]).wait()
 
@@ -387,6 +415,7 @@
     def _(i):
         normalise(i, input_rows(i))
 
+    glT[...] = gl[...].T
     for cp in const_copies[1:]:
         cp.wait()
 
@@ -453,28 +482,25 @@
         for n in "EFDUV":
             g[n + "2"].start()
 
-    def third_stage(g):
-        for n in "EFDUV":
-            g[n + "2"].forward()
-        for n in "EFD":
+    def forward_on(r, *names):
+        for n in names:
+            r[n].forward()
+
+    def third_stage(g, first="EFD", rest="UV"):
+        for n in first:
             g[n + "2"].finish()
             g[n + "3"].start()
         g["D4", 0].start()
-        for n in "UV":
+        for n in rest:
             g[n + "2"].finish()
-        g["E3"].forward()
-        g["F3"].forward()
-        for n in "UV":
             g[n + "3"].start()
 
-    def fourth_stage(g):
+    def first_quarters(g):
         g["D3"].forward()
         g["D4", 0].forward()
         g["D3"].near()
         g["D4", 1].start()
         g["D4", 2].start()
-        g["U3"].forward()
-        g["V3"].forward()
 
     def heads_ready(g):
         g["E3"].finish()
@@ -496,7 +522,13 @@
             g["D4", i].finish()
 
     second_stage(0, g0)
-    third_stage(g0)
+    forward_on(g0, "E2", "F2", "D2", "U2", "V2")
+    third_stage(g0, rest="")
+    g0["U2"].finish()
+    g0["V2"].finish()
+    forward_on(g0, "E3", "F3")
+    g0["U3"].start()
+    g0["V3"].start()
     second_stage(1, g1)
     heads_ready(g0)
 
@@ -552,6 +584,9 @@
         u1, u2 = v[:, 0:8, :], v[:, 8:16, :]
         return jnp.concatenate([u1 * cs + u2 * sn, u2 * cs - u1 * sn, v[:, 16:, :]], axis=1).reshape(heads * HD, 512)
 
+    def far_first(p, i):
+        return (p + jnp.where(i == 0, 2, jnp.where(i == 1, 1, jnp.where(i == 2, 3, 0)))) % 4
+
     def serve(i, points):
         for at, step in points.items():
             pl.when(i == at)(step)
@@ -568,7 +603,7 @@
         for k in range(4):
             acc[rows, :] += nt(act[l, k, rows, :], down_weight(l, k))
 
-    def forward(l, in_heads, before_ffn, in_ffn):
+    def forward(l, in_heads, before_ffn, in_ffn, after_hidden):
         norm_inputs(l)
         if l == 0:
             kv = nn(attn[...], key_weight()).T
@@ -582,24 +617,25 @@
         q = nn(attn[...], weight(l, Q0)) + qb
         qT[l] = rotate_heads(q.T, 6).astype(BF16)
 
-        @pl.loop(0, 12)
-        def _(i):
-            serve(i, in_heads)
-            h, b = i // 2, i % 2
+        @pl.loop(0, 6)
+        def _(h):
+            serve(h, in_heads)
             hs = pl.ds(pl.multiple_of(h * HD, HD), HD)
-            bs = pl.ds(pl.multiple_of(b * TOK, TOK), TOK)
-            s = nn(k_[bs, :], qT[l, hs, bs]) * scale + mbias[b]
-            e = jnp.exp(s - jnp.max(s, axis=0, keepdims=True))
-            low = (e * (1.0 / jnp.sum(e, axis=0, keepdims=True))).astype(BF16)
-            p_[l, h, b] = low
-            mixT[hs, bs] = nn(kvT[HD:, bs], low).astype(BF16)
+            for b in range(2):
+                bs = slice(b * TOK, (b + 1) * TOK)
+                s = nn(k_[bs, :], qT[l, hs, bs]) * scale + mbias[b]
+                e = jnp.exp(s - jnp.max(s, axis=0, keepdims=True))
+                low = (e * (1.0 / jnp.sum(e, axis=0, keepdims=True))).astype(BF16)
+                p_[l, h, b] = low
+                mixT[hs, bs] = nn(kvT[HD:, bs], low).astype(BF16)
 
         mixed[l] = mixT[...].T
         before_ffn()
 
         @pl.loop(0, 4)
-        def _(k):
-            serve(k, in_ffn)
+        def _(i):
+            k = far_first(x, i) if l == 1 else i
+            serve(i, in_ffn)
             for b in range(2):
                 rows = slice(b * TOK, (b + 1) * TOK)
                 hid = nt(mlp[rows, 0:HALF], up_weight(l, k, 0)) + nt(mlp[rows, HALF:], up_weight(l, k, 1))
@@ -608,12 +644,23 @@
                 low = (hid * phi).astype(BF16)
                 act[l, k, rows, :] = low
                 slope[l, k, rows, :] = (phi + hid * jnp.exp(-0.5 * hid * hid) * inverse_root_tau).astype(BF16)
+            after_hidden(i, k)
 
     forward(
         0,
-        {0: steps((fourth_stage, g0)), 3: steps((third_stage, g1)), 5: steps((last_quarter, g0)), 9: steps((g0["D4", 3].forward,))},
-        steps((hidden_ready, g0)),
-        {},
+        {
+            0: steps((first_quarters, g0)),
+            2: steps((forward_on, g0, "U3", "V3"), (forward_on, g1, "E2", "F2", "D2", "U2", "V2")),
+            3: steps((last_quarter, g0)),
+            5: steps((third_stage, g1)),
+        },
+        steps((forward_on, g0, ("D4", 3)), (hidden_ready, g0)),
+        {
+            1: steps((forward_on, g1, "E3", "F3")),
+            2: steps((first_quarters, g1)),
+            3: steps((forward_on, g1, "U3", "V3")),
+        },
+        lambda i, k: None,
     )
     down_ready(g0)
     swap = [to_sibling(3 + b, xs.at[b], xr.at[b]) for b in range(2)]
@@ -622,7 +669,7 @@
         xs[b] = acc[b * TOK:(b + 1) * TOK, :].astype(BF16)
         swap[b].start()
         if b == 0:
-            fourth_stage(g1)
+            last_quarter(g1)
     heads_ready(g1)
     for cp in swap:
         cp.wait()
@@ -639,96 +686,66 @@
         def _():
             h1[rows, :] = h
 
-    forward(
-        1,
-        {2: steps((last_quarter, g1)), 7: steps((g1["D4", 3].forward,))},
-        steps((hidden_ready, g1)),
-        {},
-    )
-    down_ready(g1)
-    other = pl.ds(pl.multiple_of((1 - c) * TOK, TOK), TOK)
-    down_block(1, other)
-    xs[0] = acc[other, :].astype(BF16)
-    y_copy = to_sibling(5, xs.at[0], xr.at[2])
-    y_copy.start()
-    down_block(1, own)
-    y_copy.wait()
-    out_y[...] = (h1[...] + (vec(1, 5) + vec(1, 6)) + acc[own, :] + xr[2].astype(F32)).astype(BF16)
-
     def scatters(l):
         gslot = 2 if l == 1 else 1
         g = {}
 
-        def z_then_y(i, n2, n3, row0, n, b2, b3):
-            g[n2] = Scatter(me, "z", lambda k, h: W.at[gslot, k, pl.ds(2 * h, 2), pl.ds(row0, n), :], rs_sem.at[l, i],
-                            many(n, True), b2.at[l], (2,), (n, n))
-            g[n3] = Scatter(me, "y", lambda k, h: W.at[gslot, z, k, cut(row0, n, h), :], rs_sem.at[l, i + 1],
-                            many(n, False), b3.at[l], (), halves(n))
-
-        def y_then_z(i, n2, n3, row0, n, b2, b3):
-            g[n2] = Scatter(me, "y", lambda k, h: W.at[gslot, pl.ds(2 * h, 2), k, pl.ds(row0, n), :], rs_sem.at[l, i],
-                            many(n, True), b2.at[l], (2,), (n, n))
-            g[n3] = Scatter(me, "z", lambda k, h: W.at[gslot, k, y, cut(row0, n, h), :], rs_sem.at[l, i + 1],
-                            many(n, False), b3.at[l], (), halves(n))
-
-        for i, dz in enumerate((2, 1, 3, 0)):
-            g["D1", i] = Scatter(me, "x", lambda k, h, dz=dz: W.at[gslot, (z + dz) % 4, pl.ds(2 * h, 2), pl.ds(quarter(k), 48), :],
+        def y_then_z(i, name, row0, n, b2, b3):
+            g[name + "2"] = Scatter(me, "y", lambda k, h: W.at[gslot, pl.ds(2 * h, 2), k, pl.ds(row0, n), :],
+                                    rs_sem.at[l, i], many(n, True), b2.at[l], (2,), (n, n))
+            g[name + "3"] = Direct(me, "z", lambda k: W.at[gslot, k, y, pl.ds(row0, n), :], rs_sem.at[l, i + 1],
+                                   many(n, False), b3.at[l, :, pl.ds(0, n)])
+
+        for i, dy in enumerate((2, 1, 3, 0)):
+            g["D1", i] = Scatter(me, "x", lambda k, h, dy=dy: W.at[gslot, pl.ds(2 * h, 2), (y + dy) % 4, pl.ds(quarter(k), 48), :],
                                  rs_sem.at[l, i], many(48, True), bD1.at[l, i], (2,), (48, 48))
-        z_then_y(4, "D2", "D3", quarter(x), 48, bD2, bD3)
-        y_then_z(6, "O2", "O3", O0, 48, bO2, bO3)
-        z_then_y(8, "U2", "U3", U0, 96, bU2, bU3)
-        y_then_z(14, "V2", "V3", U0 + 96, 96, bV2, bV3)
+        y_then_z(4, "D", quarter(x), 48, bD2, bD3)
+        y_then_z(6, "O", O0, 48, bO2, bO3)
         a0 = 0 if l == 0 else VEC0
-        z_then_y(10, "A2", "A3", a0, 48 - a0, bA2, bA3)
-        y_then_z(12, "B2", "B3", 48, 32, bB2, bB3)
+        y_then_z(8, "A", a0, 48 - a0, bA2, bA3)
+        y_then_z(10, "B", 48, 32, bB2, bB3)
+        g["U2"] = Scatter(me, "z", lambda k, h: W.at[gslot, k, pl.ds(2 * h, 2), pl.ds(U0, 192), :], rs_sem.at[l, 12],
+                          many(192, True), bU2.at[l], (2,), (192, 192))
+        g["U3"] = Scatter(me, "y", lambda k, h: W.at[gslot, z, k, cut(U0, 192, h), :], rs_sem.at[l, 13],
+                          many(192, False), bU3.at[l], (), (96, 96))
         return g
 
     def finish_line(l):
-        gslot = 2 if l == 1 else 1
-        B = W.at[gslot, z, y]
-        rowd = lax.broadcasted_iota(jnp.int32, (288, HALF), 0)
-        lo = 96 + 48 * x
-        blk = B[Q0:U0, :].astype(F32)
-        blk = jnp.where((rowd < 96) | ((rowd >= lo) & (rowd < lo + 48)), blk, 0.0).astype(BF16)
-        stack = nn(c_qodT[...], blk)
+        B = W.at[2 if l == 1 else 1, z, y]
+        rows = jnp.concatenate([B[Q0:D0, :], B[pl.ds(quarter(x), 48), :], B[VEC0:VEC0 + 16, :]], axis=0)
+        stack = nn(c_sums[...], rows)
         if l == 0:
             kv = B[KV0:KV0 + 16, :]
             kv = jnp.concatenate([kv[:, 0:128], kv[:, 128:256], kv[:, 256:384]], axis=0)
-            stack = stack + jnp.concatenate([nn(c_kvT[...], kv), jnp.zeros((512, 256), F32)], axis=1)
-        stack = stack.astype(BF16).reshape(8, CHUNK, HALF)
-        got[l] = stack
-        for s in range(8):
-            got[l, s, 0:16, :] = B[VEC0:VEC0 + 16, :]
+            stack = stack + jnp.concatenate([nn(c_sums_kv[...], kv), jnp.zeros((256, 256), F32)], axis=1)
+        back[l] = stack.astype(BF16).reshape(8, 32, HALF)
         gotu[l] = nn(c_upT[...], B[U0:ROWS, :]).astype(BF16).reshape(4, 48, HALF)
-        line_copies(l, lambda s, t: got.at[l, s], rgot, lambda xx: gotu.at[l, xx], rgotu, line_sem.at[2 + l])
-        rgot[l, s_me] = got[l, s_me]
+        line_copies(l, lambda s, t: back.at[l, s], rgot, lambda xx: gotu.at[l, xx], rgotu, line_sem.at[2 + l])
+        rgot[l, s_me] = back[l, s_me]
         rgotu[l, x] = gotu[l, x]
 
     def last_sums(l):
-        line_wait(line_sem.at[2 + l])
-        halves = []
+        line_wait(line_sem.at[2 + l], 32)
+        halves, tiles = [], []
         for t in range(2):
-            v = rgot[l, t].astype(F32)
-            for xx in range(1, 4):
-                v = v + rgot[l, 2 * xx + t].astype(F32)
-            halves.append(v)
-        v = jnp.concatenate(halves, axis=1)
-        hi = v.astype(BF16)
-        lo = (v - hi.astype(F32)).astype(BF16)
-        unperm = nt(hi, c_perm[...]) + nt(lo, c_perm[...])
-        row = lax.broadcasted_iota(jnp.int32, (CHUNK, HALF), 0)
-        lane = lax.broadcasted_iota(jnp.int32, (CHUNK, HALF), 1)
+            parts = [rgot[l, 2 * xx + t].astype(F32) for xx in range(4)]
+            halves.append(parts[0] + parts[1] + parts[2] + parts[3])
+        for xx in range(4):
+            tiles.append(jnp.concatenate([rgot[l, 2 * xx, 0:32, :], rgot[l, 2 * xx + 1, 0:32, :]], axis=1))
+        unperm = nt(jnp.concatenate(tiles, axis=0), c_perm[...])
+        row = lax.broadcasted_iota(jnp.int32, (32, HALF), 0)
+        lane = lax.broadcasted_iota(jnp.int32, (32, HALF), 1)
         both = halves[0] + halves[1]
         mine = jnp.where(lane < 128, both, jnp.where(c == 0, halves[0], halves[1]))
         hi = mine.astype(BF16)
         lo = (mine - hi.astype(F32)).astype(BF16)
-        lp = lane_place()
-        small = nt(hi, lp) + nt(lo, lp)
-        first = jnp.where(row < 34, halves[0], unperm[:, 0:HALF])
-        first = jnp.where(row < 22, both, first)
-        out_v[l, :, 0:HALF] = first
-        out_v[l, :, HALF:] = jnp.where(row < 34, halves[1], unperm[:, HALF:])
-        out_v[l, 0:16, 0:128] = small[0:16]
+        spot = lane_place()
+        small = nt(hi, spot) + nt(lo, spot)
+        out_v[l, 0:32, 0:HALF] = jnp.where(row < 18, halves[0], both)
+        out_v[l, 0:32, HALF:] = halves[1]
+        out_v[l, 24:32, 0:128] = small[24:32]
+        for xx in range(4):
+            out_v[l, 32 + 16 * xx:48 + 16 * xx, :] = unperm[32 * xx + 8:32 * xx + 24]
         u = rgotu[l, 0].astype(F32)
         for xx in range(1, 4):
             u = u + rgotu[l, xx].astype(F32)
@@ -740,10 +757,6 @@
         for i in range(4):
             r["D1", i].start()
         r["O2"].start()
-
-    def forward_on(r, *names):
-        for n in names:
-            r[n].forward()
 
     def next_ring(r, *names):
         for n in names:
@@ -762,34 +775,30 @@
         for n in names:
             r[n].finish()
 
-    def backward(l, r, after_norm, after_down, in_ffn, before_heads, in_heads, before_query):
-        gslot = 2 if l == 1 else 1
-        G = W.at[gslot]
-        after_norm()
-        glT[...] = gl[...].T
-        vg[5:6, :] = jnp.sum(gl[own, :].astype(F32), axis=0, keepdims=True)
-
+    def out_grad(l):
         for b in range(2):
             rows = slice(b * HALF, (b + 1) * HALF)
             part = nn(glT[rows, :], mixed[l]).astype(BF16).reshape(2, 4, 48, HALF)
-            G[2 * b:2 * b + 2, :, O0:O0 + 48, :] = part
-
+            W[2 if l == 1 else 1, 2 * b:2 * b + 2, :, O0:O0 + 48, :] = part
+
+    def down_grad(l, r, i, k):
+        rows_d = pl.ds(pl.multiple_of(D0 + 48 * k, 16), 48)
+        for b in range(2):
+            rows = slice(b * HALF, (b + 1) * HALF)
+            part = nn(glT[rows, :], act[l, k]).astype(BF16).reshape(2, 4, 48, HALF)
+            W[2 if l == 1 else 1, 2 * b:2 * b + 2, :, rows_d, :] = part
+        rings = [r["D1", j] for j in range(4)]
+        serve(i, {0: steps(*((ring.start_far,) for ring in rings)), 2: steps(*((ring.start_near,) for ring in rings))})
+
+    def backward(l, r, in_ffn, before_heads, in_heads, before_query):
+        G = W.at[2 if l == 1 else 1]
+        vg[5:6, :] = jnp.sum(gl[own, :].astype(F32), axis=0, keepdims=True)
         acc[...] = jnp.zeros_like(acc)
 
         @pl.loop(0, 4)
-        def _(k):
-            rows_d = pl.ds(pl.multiple_of(D0 + 48 * k, 16), 48)
-            for b in range(2):
-                rows = slice(b * HALF, (b + 1) * HALF)
-                part = nn(glT[rows, :], act[l, k]).astype(BF16).reshape(2, 4, 48, HALF)
-                G[2 * b:2 * b + 2, :, rows_d, :] = part
-
-        first_sums(r)
-        after_down()
-
-        @pl.loop(0, 4)
-        def _(k):
-            serve(k, in_ffn)
+        def _(i):
+            k = far_first(z, i)
+            serve(i, in_ffn)
             sums = jnp.zeros((1, HALF), F32)
             for b in range(2):
                 rows = slice(b * TOK, (b + 1) * TOK)
@@ -804,9 +813,8 @@
             for h in range(2):
                 part = nn(ghT, mlp[:, h * HALF:(h + 1) * HALF]).astype(BF16).reshape(4, 96, HALF)
                 G[k, :, U0 + 96 * h:U0 + 96 * h + 96, :] = part
-
-        r["U2"].start()
-        r["V2"].start()
+            serve(i, {0: r["U2"].start_far, 2: r["U2"].start_near})
+
         before_heads()
 
         for b in range(2):
@@ -818,23 +826,23 @@
             dk[...] = jnp.zeros_like(dk)
             dv[...] = jnp.zeros_like(dv)
 
-        @pl.loop(0, 12)
-        def _(i):
-            h, b = i // 2, i % 2
+        @pl.loop(0, 6)
+        def _(h):
+            serve(h, in_heads)
             hs = pl.ds(pl.multiple_of(h * HD, HD), HD)
-            bs = pl.ds(pl.multiple_of(b * TOK, TOK), TOK)
-            serve(i, in_heads)
-            low = p_[l, h, b]
-            probs = low.astype(F32)
-            t = probs * nn(v_[bs, :], gmT[hs, bs])
-            grad = (t - probs * jnp.sum(t, axis=0, keepdims=True)).astype(BF16)
-            dq = nn(kvT[0:HD, bs], grad) * scale
-            cs, sn = cosT[:, bs], sinT[:, bs]
-            u1, u2 = dq[0:8], dq[8:16]
-            dq = jnp.concatenate([u1 * cs + u2 * sn, u2 * cs - u1 * sn, dq[16:]], axis=0)
-            mixT[hs, bs] = dq.astype(BF16)
-            dk[bs, :] += nt(grad, qT[l, hs, bs])
-            dv[bs, :] += nt(low, gmT[hs, bs])
+            for b in range(2):
+                bs = slice(b * TOK, (b + 1) * TOK)
+                low = p_[l, h, b]
+                probs = low.astype(F32)
+                t = probs * nn(v_[bs, :], gmT[hs, bs])
+                grad = (t - probs * jnp.sum(t, axis=0, keepdims=True)).astype(BF16)
+                dq = nn(kvT[0:HD, bs], grad) * scale
+                cs, sn = cosT[:, bs], sinT[:, bs]
+                u1, u2 = dq[0:8], dq[8:16]
+                dq = jnp.concatenate([u1 * cs + u2 * sn, u2 * cs - u1 * sn, dq[16:]], axis=0)
+                mixT[hs, bs] = dq.astype(BF16)
+                dk[bs, :] += nt(grad, qT[l, hs, bs])
+                dv[bs, :] += nt(low, gmT[hs, bs])
 
         before_query()
         low = mixT[...].T
@@ -858,17 +866,18 @@
             G[:, :, KV0:KV0 + 16, :] = jnp.concatenate([dkv[:, :, 0:16], dkv[:, :, 16:32], dkv[:, :, 32:48]], axis=3)
 
     def fold_block(l, b, sums):
+        hold = g_ if l == 1 else h1
         rows = slice(b * TOK, (b + 1) * TOK)
         ea = nt(gm[rows, :], weight(l, Q0))
         if l == 0:
             ea = ea + nt(gs[rows, :], key_weight())
-        h1[...] = ea
+        hold[...] = ea
 
         def fold(i, sums):
             rows = pl.ds(pl.multiple_of(i * CH, CH), CH)
             all_rows = pl.ds(pl.multiple_of(b * TOK + i * CH, CH), CH)
             n = n_[all_rows, :] if l == 1 else norm_of(X2[b, rows, :].astype(F32))[0]
-            ea, em = h1[rows, :], acc[all_rows, :]
+            ea, em = hold[rows, :], acc[all_rows, :]
             xs[b, rows, :] = (ea * vec(l, 0) + em * vec(l, 1)).astype(BF16)
             add = [ea * n, em * n, ea, em]
             return tuple(s + jnp.sum(a, axis=0, keepdims=True) for s, a in zip(sums, add))
@@ -901,33 +910,43 @@
 
     no_sums = (jnp.zeros((1, D), F32),) * 4
 
+    forward(
+        1,
+        {1: steps((g1["D4", 3].forward,))},
+        steps((out_grad, 1), (r1["O2"].start,), (hidden_ready, g1)),
+        {},
+        lambda i, k: down_grad(1, r1, i, k),
+    )
     attnT[...] = attn[...].T
+    down_ready(g1)
     backward(
-        1, r1, steps(), steps(),
-        {3: steps((forward_on, r1, ("D1", 0), "O2"))},
-        steps((forward_on, r1, ("D1", 1))),
-        {4: steps((next_ring, r1, "O"), (forward_on, r1, ("D1", 2))), 9: steps((forward_on, r1, ("D1", 3)))},
-        steps((forward_on, r1, "U2", "V2", "O3")),
+        1, r1,
+        {1: steps((forward_on, r1, "O2")), 3: steps((forward_on, r1, ("D1", 0)))},
+        steps((forward_on, r1, ("D1", 1)), (next_ring, r1, "O")),
+        {2: steps((forward_on, r1, ("D1", 2))), 4: steps((forward_on, r1, ("D1", 3)))},
+        steps((forward_on, r1, "U2")),
     )
-    swap = [to_sibling(6 + b, xs.at[b], xr.at[b]) for b in range(2)]
+    swap = [to_sibling(6 + b, xs.at[b], xr.at[2 + b]) for b in range(2)]
     sums = no_sums
     for b in range(2):
         sums = fold_block(1, b, sums)
         swap[b].start()
     query_grad(1, r1)
     vector_grad(1, r1, sums)
-    r1["O3"].finish()
-    norm_inputs(0, again=True)
-    attnT[...] = attn[...].T
-    down_second(r1)
+    other = pl.ds(pl.multiple_of((1 - c) * TOK, TOK), TOK)
+    down_block(1, other)
+    xs[2] = acc[other, :].astype(BF16)
+    y_copy = to_sibling(5, xs.at[2], xr.at[0])
+    down_block(1, own)
     for cp in swap:
         cp.wait()
+    y_copy.start()
 
     @pl.loop(0, 8)
     def _(i):
         b = i // 4
         rows = pl.ds(pl.multiple_of((i % 4) * CH, CH), CH)
-        s = xs[b, rows, :].astype(F32) + xr[b, rows, :].astype(F32)
+        s = xs[b, rows, :].astype(F32) + xr[2 + b, rows, :].astype(F32)
         all_rows = pl.ds(pl.multiple_of(i * CH, CH), CH)
         g = through_norm(n_[all_rows, :], r_[all_rows, 0:1], gl[all_rows, :].astype(F32), s)
         gl[all_rows, :] = g.astype(BF16)
@@ -936,49 +955,67 @@
         def _():
             g_[rows, :] = g
 
+    down_second(r1)
+    forward_on(r1, "A2", "B2")
+    glT[...] = gl[...].T
+
+    @pl.loop(0, 4)
+    def _(i):
+        down_grad(0, r0, i, far_first(x, i))
+
+    out_grad(0)
+    r0["O2"].start()
+    norm_inputs(0, again=True)
+    attnT[...] = attn[...].T
+    y_copy.wait()
+    out_y[...] = (h1[...] + (vec(1, 5) + vec(1, 6)) + acc[own, :] + xr[0].astype(F32)).astype(BF16)
     backward(
         0, r0,
-        steps((forward_on, r1, "A2", "B2")),
-        steps((forward_on, r1, "D2")),
         {
-            1: steps((next_ring, r1, "U", "V")),
-            2: steps((next_ring, r1, "A", "B", "D")),
-            3: steps((forward_on, r1, "U3", "V3")),
+            1: steps((forward_on, r0, "O2")),
+            2: steps((next_ring, r1, "U"), (forward_on, r1, "D2")),
+            3: steps((next_ring, r1, "A", "B"), (forward_on, r0, ("D1", 0))),
         },
-        steps((forward_on, r0, ("D1", 0), "O2"), (forward_on, r1, "A3", "B3", "D3")),
+        steps((forward_on, r0, ("D1", 1))),
         {
-            3: steps((forward_on, r0, ("D1", 1))),
-            6: steps((forward_on, r0, ("D1", 2)), (next_ring, r0, "O")),
-            10: steps((forward_on, r0, ("D1", 3))),
+            0: steps((next_ring, r0, "O")),
+            1: steps((forward_on, r0, ("D1", 2))),
+            2: steps((next_ring, r1, "D"), (forward_on, r1, "U3")),
+            3: steps((forward_on, r0, "U2", ("D1", 3))),
         },
-        steps((forward_on, r0, "U2", "V2", "O3")),
+        steps(),
     )
     query_grad(0, r0)
     sums = no_sums
     for b in range(2):
         sums = fold_block(0, b, sums)
-    swap = to_sibling(8, xs.at[1 - c], xr.at[2])
+    swap = to_sibling(8, xs.at[1 - c], xr.at[1])
     swap.start()
+    r0["D1", 0].finish()
+    r0["D2"].start_far()
     vector_grad(0, r0, sums)
-    finish_third(r1, ("U3", "V3", "A3", "B3", "D3"))
+    r0["D1", 1].finish()
+    r0["D1", 2].finish()
+    r0["D2"].start_near()
+    r0["D1", 3].finish()
+    forward_on(r0, "B2")
+    next_ring(r0, "U")
+    finish_third(r1, ("O3", "A3", "B3", "D3", "U3"))
     finish_line(1)
+    forward_on(r0, "A2", "D2")
+    next_ring(r0, "B", "A", "D")
+    forward_on(r0, "U3")
     swap.wait()
 
     @pl.loop(0, 4)
     def _(i):
         rows = pl.ds(pl.multiple_of(i * CH, CH), CH)
-        s = xs[c, rows, :].astype(F32) + xr[2, rows, :].astype(F32)
+        s = xs[c, rows, :].astype(F32) + xr[1, rows, :].astype(F32)
         n, inverse = norm_of(X2[c, rows, :].astype(F32))
         out_gx[rows, :] = through_norm(n, inverse, g_[rows, :], s).astype(BF16)
 
-    forward_on(r0, "B2", "A2")
-    down_second(r0)
-    next_ring(r0, "U", "V", "B", "A")
-    forward_on(r0, "D2", "U3", "V3")
-    next_ring(r0, "D")
-    forward_on(r0, "B3", "A3", "D3")
     last_sums(1)
-    finish_third(r0, ("O3", "U3", "V3", "A3", "B3", "D3"))
+    finish_third(r0, ("O3", "U3", "B3", "A3", "D3"))
     finish_line(0)
     last_sums(0)
 
@@ -998,14 +1035,14 @@
         vmem(HALF, T2), vmem(2, T2, HALF), vmem(2, 4, T2, HALF), vmem(2, 4, T2, HALF),
         vmem(T2, D, dtype=F32), vmem(D, T2), vmem(D, T2), vmem(T2, HALF), vmem(HALF, T2),
         vmem(T2, HD, dtype=F32), vmem(T2, HD, dtype=F32), vmem(T2, 128), vmem(16, D, dtype=F32),
-        vmem(4, 8, HALF, dtype=F32), vmem(TOK, D, dtype=F32), vmem(2, TOK, D), vmem(3, TOK, D),
-        vmem(2, 6, 2, 48, HALF), vmem(2, 6, 2, 32, HALF), vmem(2, 6, 2, 48, HALF), vmem(2, 6, 2, 96, HALF), vmem(2, 6, 2, 96, HALF),
+        vmem(4, 8, HALF, dtype=F32), vmem(TOK, D, dtype=F32), vmem(3, TOK, D), vmem(4, TOK, D),
+        vmem(2, 6, 2, 48, HALF), vmem(2, 6, 2, 32, HALF), vmem(2, 6, 2, 48, HALF), vmem(2, 6, 2, 192, HALF),
         vmem(2, 4, 6, 2, 48, HALF), vmem(2, 6, 2, 48, HALF),
-        vmem(2, 6, 32, HALF), vmem(2, 6, 16, HALF), vmem(2, 6, 32, HALF), vmem(2, 6, 48, HALF), vmem(2, 6, 48, HALF), vmem(2, 6, 32, HALF),
-        vmem(2, 8, CHUNK, HALF), vmem(2, 4, 48, HALF),
+        vmem(2, 3, 48, HALF), vmem(2, 3, 32, HALF), vmem(2, 3, 48, HALF), vmem(2, 6, 96, HALF), vmem(2, 3, 48, HALF),
+        vmem(2, 8, 32, HALF), vmem(2, 8, 32, HALF), vmem(2, 4, 48, HALF),
         *[vmem(*v.shape) for v in (CONSTS[i] for i in range(9))],
         pltpu.SemaphoreType.DMA((9,)), pltpu.SemaphoreType.DMA((9,)), pltpu.SemaphoreType.DMA((9,)),
-        pltpu.SemaphoreType.DMA((4, 4)), pltpu.SemaphoreType.DMA((2, 14, 5)), pltpu.SemaphoreType.DMA((2, 16, 4)),
+        pltpu.SemaphoreType.DMA((4, 4)), pltpu.SemaphoreType.DMA((2, 14, 5)), pltpu.SemaphoreType.DMA((2, 14, 4)),
     ]
     whole = pl.BlockSpec(memory_space=pltpu.VMEM)
     return pl.pallas_call(
@@ -1013,7 +1050,7 @@
         out_shape=(
             jax.ShapeDtypeStruct((TOK, D), BF16),
             jax.ShapeDtypeStruct((TOK, D), BF16),
-            jax.ShapeDtypeStruct((2, CHUNK, D), F32),
+            jax.ShapeDtypeStruct((2, 96, D), F32),
             jax.ShapeDtypeStruct((2, 48, HALF), F32),
         ),
         in_specs=[whole] * 14 + [pl.BlockSpec(memory_space=pl.ANY)] * 9,
@@ -1033,20 +1070,21 @@
     o_y[...] = y[...]
     o_gx[...] = gx[...]
     for l in range(2):
-        o_gain[l] = v[l, 0:2, 0:6]
-        o_nbias[l] = v[l, 2:4, 0:6]
-        o_qb[l:l + 1, :] = v[l, 4:5, 0:6]
-        o_ob[l:l + 1, :] = v[l, 5:6, 0:6]
-        o_db[l:l + 1, :] = v[l, 5:6, 0:6]
-        o_ub[l:l + 1, :] = v[l, 6:7, 8:32]
+        o_gain[l] = v[l, 24:26, 0:6]
+        o_nbias[l] = v[l, 26:28, 0:6]
+        o_qb[l:l + 1, :] = v[l, 28:29, 0:6]
+        o_ob[l:l + 1, :] = v[l, 29:30, 0:6]
+        o_db[l:l + 1, :] = v[l, 29:30, 0:6]
+        o_ub[l:l + 1, :] = v[l, 30:31, 8:32]
         for h in range(2):
             o_up[l, :, h * HALF:(h + 1) * HALF] = u[l, 24 * h:24 * h + 24, :]
         for i in range(6):
-            o_q[i, l:l + 1, :] = v[l, 22 + i:23 + i, :]
-            o_o[i, l:l + 1, :] = v[l, 28 + i:29 + i, :]
+            o_q[i, l:l + 1, :] = v[l, i:i + 1, :]
+            o_o[i, l:l + 1, :] = v[l, 6 + i:7 + i, :]
             for g in range(4):
-                o_down[i, l:l + 1, g * D:(g + 1) * D] = v[l, 34 + 4 * i + g:35 + 4 * i + g, :]
-    o_kv[...] = v[0, 16:22, 0:128]
+                at = 32 + 16 * g + 4 + i
+                o_down[i, l:l + 1, g * D:(g + 1) * D] = v[l, at:at + 1, :]
+    o_kv[...] = v[0, 18:24, 0:128]
 
 
 def pack(y, gx, v, u):

time: 178 us -> 166 us (0.933)
  Pallas kernels: 176 us -> 165 us
    pallas_call x1, Pallas kernels: 174 us -> 163 us  [on_device(): make_call()]
where the time goes in v2:
time: 166 us
  Pallas kernels  165 us (99%)
    pallas_call x1, Pallas kernels, on_device(): make_call()  163 us

profile of v2, /device:TPU:1, one launch (start us, length us, event | category | flops | bytes accessed | tf_op | source)
XLA Modules:
  0.0 166.0 jit_solution(5582602440875431240)
XLA Ops:
  0.7 162.8 %two_layers.1 = (bf16[256,768]{1,0:T(8,128)(2,1)}, bf16[256,768]{1,0:T(8,128)(2,1)}, f32[2,96,768]{2,1,0:T(8,128)}, f32[2,48,384]{2,1,0:T(8,128)}) custom-call(bf16[256,768]{1,0:T(8,128)(2,1)} %xin.1, s32[1,256]{1,0:T(1,128)} %seg.1, bf16[256,768]{1,0:T(8,128)(2,1)} %cot.1, bf16[2,2,6]{2,1,0:T(2,128)(2,1)} %w_gain.1, bf16[2,2,6]{2,1,0:T(2,128)(2,1)} %w_nbias.1, ...), custom_call_target="tpu_custom_call" | custom-call | tf_op jit(solution)/shard_map/two_layers/pallas_call | solution.py:1108
  163.4 2.4 %results.1 = (bf16[256,768]{1,0:T(8,128)(2,1)}, bf16[256,768]{1,0:T(8,128)(2,1)}, f32[2,2,6]{2,1,0:T(2,128)}, f32[2,2,6]{2,1,0:T(2,128)}, f32[6,2,768]{2,1,0:T(2...) custom-call(bf16[256,768]{1,0:T(8,128)(2,1)} %get-tuple-element.30.y, ...), custom_call_target="tpu_custom_call" | custom-call | tf_op jit(solution)/shard_map/results/pallas_call | solution.py:1093

commit v3 on v2

--- a/solution.py
+++ b/solution.py
@@ -617,9 +617,11 @@
         q = nn(attn[...], weight(l, Q0)) + qb
         qT[l] = rotate_heads(q.T, 6).astype(BF16)
 
-        @pl.loop(0, 6)
-        def _(h):
-            serve(h, in_heads)
+        @pl.loop(0, 3)
+        def _(pair):
+          serve(2 * pair, in_heads)
+          serve(2 * pair + 1, in_heads)
+          for h in (2 * pair, 2 * pair + 1):
             hs = pl.ds(pl.multiple_of(h * HD, HD), HD)
             for b in range(2):
                 bs = slice(b * TOK, (b + 1) * TOK)
@@ -652,7 +654,7 @@
             0: steps((first_quarters, g0)),
             2: steps((forward_on, g0, "U3", "V3"), (forward_on, g1, "E2", "F2", "D2", "U2", "V2")),
             3: steps((last_quarter, g0)),
-            5: steps((third_stage, g1)),
+            4: steps((third_stage, g1)),
         },
         steps((forward_on, g0, ("D4", 3)), (hidden_ready, g0)),
         {
@@ -826,9 +828,11 @@
             dk[...] = jnp.zeros_like(dk)
             dv[...] = jnp.zeros_like(dv)
 
-        @pl.loop(0, 6)
-        def _(h):
-            serve(h, in_heads)
+        @pl.loop(0, 3)
+        def _(pair):
+          serve(2 * pair, in_heads)
+          serve(2 * pair + 1, in_heads)
+          for h in (2 * pair, 2 * pair + 1):
             hs = pl.ds(pl.multiple_of(h * HD, HD), HD)
             for b in range(2):
                 bs = slice(b * TOK, (b + 1) * TOK)

time: 166 us -> 165 us (level)
  no operation moved by 1% of the time
where the time goes in v3:
time: 165 us
  Pallas kernels  164 us (99%)
    pallas_call x1, Pallas kernels, on_device(): make_call()  162 us

profile of v3, /device:TPU:1, one launch (start us, length us, event | category | flops | bytes accessed | tf_op | source)
XLA Modules:
  0.0 164.7 jit_solution(12097959262732199164)
XLA Ops:
  0.7 161.5 %two_layers.1 = (bf16[256,768]{1,0:T(8,128)(2,1)}, bf16[256,768]{1,0:T(8,128)(2,1)}, f32[2,96,768]{2,1,0:T(8,128)}, f32[2,48,384]{2,1,0:T(8,128)}) custom-call(bf16[256,768]{1,0:T(8,128)(2,1)} %xin.1, s32[1,256]{1,0:T(1,128)} %seg.1, bf16[256,768]{1,0:T(8,128)(2,1)} %cot.1, bf16[2,2,6]{2,1,0:T(2,128)(2,1)} %w_gain.1, bf16[2,2,6]{2,1,0:T(2,128)(2,1)} %w_nbias.1, ...), custom_call_target="tpu_custom_call" | custom-call | tf_op jit(solution)/shard_map/two_layers/pallas_call | solution.py:1112
  162.2 2.4 %results.1 = (bf16[256,768]{1,0:T(8,128)(2,1)}, bf16[256,768]{1,0:T(8,128)(2,1)}, f32[2,2,6]{2,1,0:T(2,128)}, f32[2,2,6]{2,1,0:T(2,128)}, f32[6,2,768]{2,1,0:T(2...) custom-call(bf16[256,768]{1,0:T(8,128)(2,1)} %get-tuple-element.30.y, ...), custom_call_target="tpu_custom_call" | custom-call | tf_op jit(solution)/shard_map/results/pallas_call | solution.py:1097

commit v4 on v3

--- a/solution.py
+++ b/solution.py
@@ -287,13 +287,13 @@
         wide = (r >= 8) & (r < 32) & (m == r - 8 + 128 + 24 * x)
         return jnp.where(small | wide, 1.0, 0.0).astype(BF16)
 
-    def line_copies(l, bufs, into, bufu, intou, sems):
+    def line_copies(l, bufs, into, bufu, intou, sems, rows=slice(None)):
         out = []
         for dx, dc in line:
             t = (c + dc) % 2
             s_to = ((x + dx) % 4) * 2 + t
             out.append(pltpu.make_async_remote_copy(
-                src_ref=bufs(s_to, t), dst_ref=into.at[l, s_me], send_sem=sems.at[0], recv_sem=sems.at[1],
+                src_ref=bufs(s_to, t), dst_ref=into.at[l, s_me, rows], send_sem=sems.at[0], recv_sem=sems.at[1],
                 device_id=me.dev(dx=dx, dc=dc), device_id_type=MESH))
         for dx in range(1, 4):
             out.append(pltpu.make_async_remote_copy(
@@ -346,8 +346,12 @@
             chunk[l, t] = part.astype(BF16)
 
     def send_chunks(l):
-        line_copies(l, lambda s, t: chunk.at[l, t], got, lambda xx: rawu.at[l], gotu, line_sem.at[l])
-        got[l, s_me] = chunk[l, c]
+        first = 0 if l == 0 else 16
+        rows = pl.ds(first, CHUNK - first)
+        line_copies(l, lambda s, t: chunk.at[l, t, rows], got, lambda xx: rawu.at[l], gotu, line_sem.at[l], rows)
+        if l == 1:
+            got[l, :, 0:16, :] = jnp.zeros((8, 16, HALF), BF16)
+        got[l, s_me, rows] = chunk[l, c, rows]
         gotu[l, x] = rawu[l]
 
     prepare(0)
@@ -423,7 +427,7 @@
         return pl.multiple_of(D0 + 48 * k, 16)
 
     def assemble(l):
-        line_wait(line_sem.at[l])
+        line_wait(line_sem.at[l], CHUNK if l == 0 else CHUNK - 16)
         stack = got[l].reshape(512, HALF)
         W[l, z, y, Q0:D0, :] = nn(c_qod[0:96, :], stack).astype(BF16)
         down = nn(c_qod[pl.ds(pl.multiple_of(96 + 48 * x, 16), 48), :], stack).astype(BF16)

time: 165 us -> 166 us (level)
  no operation moved by 1% of the time
where the time goes in v4:
time: 166 us
  Pallas kernels  165 us (99%)
    pallas_call x1, Pallas kernels, on_device(): make_call()  162 us

profile of v4, /device:TPU:1, one launch (start us, length us, event | category | flops | bytes accessed | tf_op | source)
XLA Modules:
  0.0 165.6 jit_solution(767729082433841886)
XLA Ops:
  0.7 162.4 %two_layers.1 = (bf16[256,768]{1,0:T(8,128)(2,1)}, bf16[256,768]{1,0:T(8,128)(2,1)}, f32[2,96,768]{2,1,0:T(8,128)}, f32[2,48,384]{2,1,0:T(8,128)}) custom-call(bf16[256,768]{1,0:T(8,128)(2,1)} %xin.1, s32[1,256]{1,0:T(1,128)} %seg.1, bf16[256,768]{1,0:T(8,128)(2,1)} %cot.1, bf16[2,2,6]{2,1,0:T(2,128)(2,1)} %w_gain.1, bf16[2,2,6]{2,1,0:T(2,128)(2,1)} %w_nbias.1, ...), custom_call_target="tpu_custom_call" | custom-call | tf_op jit(solution)/shard_map/two_layers/pallas_call | solution.py:1116
  163.0 2.4 %results.1 = (bf16[256,768]{1,0:T(8,128)(2,1)}, bf16[256,768]{1,0:T(8,128)(2,1)}, f32[2,2,6]{2,1,0:T(2,128)}, f32[2,2,6]{2,1,0:T(2,128)}, f32[6,2,768]{2,1,0:T(2...) custom-call(bf16[256,768]{1,0:T(8,128)(2,1)} %get-tuple-element.30.y, ...), custom_call_target="tpu_custom_call" | custom-call | tf_op jit(solution)/shard_map/results/pallas_call | solution.py:1101
